TPU v7x, 256 devices: a whole 4x4x8 slice. The times are simulated.
256 devices in a mesh: section: 8 (over x, z_hi), dp: 32 (over z_lo, y, core).
Axes of the slice: x: 4, y: 4, z: 8 (z_hi: 2, z_lo: 4; z = z_hi * 4 + z_lo), core: 2. Of those that a mesh axis runs over, the one named last changes fastest.
Arguments:
- text: bfloat16 [6144, 8192], P('dp'), may hold values from -60 to 60
- image: bfloat16 [1536, 3200], P('dp'), may hold values from -60 to 60
- positions: int32 [96, 16], P('dp'), may hold values from 0 to 63, as said below
- enc_in: bfloat16 [8, 3200, 128], P('section', 'dp'), may hold values from -0.109375 to 0.109375
- enc_out: bfloat16 [8, 128, 3200], P('section', None, 'dp'), may hold values from -0.5 to 0.5
- conn_in: bfloat16 [3200, 64], P('dp'), may hold values from -0.109375 to 0.109375
- conn_out: bfloat16 [64, 8192], P(None, 'dp'), may hold values from -0.75 to 0.75
- llm_in: bfloat16 [8, 8192, 512], P('section', 'dp'), may hold values from -0.0625 to 0.0625
- llm_out: bfloat16 [8, 512, 8192], P('section', None, 'dp'), may hold values from -0.25 to 0.25
Outputs:
- layer_states: bfloat16 [8, 6144, 8192], P('section', 'dp')
Inputs may be any that keep to these rules, and one draw needn't show every extreme that they name: Each row holds 16 distinct positions within one micro-batch of 64 rows, in ascending order.
All inputs are finite; a program needn't handle non-finite values.
Results may differ from a plain program's by a relative error of at most 0.009.
Values may be sent and summed in bfloat16 or wider, within the bound.
A program may use at most 128 MiB of HBM per device.

v0:
```python
import jax
import jax.numpy as jnp
from jax import lax
from jax.sharding import PartitionSpec as P

EPSILON = 1e-06


def copy_for_each(x, axis):
    copies = jnp.broadcast_to(x, (lax.axis_size(axis), *x.shape))
    return lax.all_to_all(copies, axis, split_axis=0, concat_axis=0, tiled=True)


def laid_out(blocks, dim):
    blocks = jnp.moveaxis(blocks, 0, dim)
    lengths = blocks.shape
    return blocks.reshape(*lengths[:dim], lengths[dim] * lengths[dim + 1], *lengths[dim + 2 :])


def gathered_copies(x, axis, dim):
    blocks = copy_for_each(x, axis)
    return laid_out(blocks, dim)


def rows_first(arrays, axis, dims):
    turned = [jnp.moveaxis(a, dim, 0) for a, dim in zip(arrays, dims)]
    widths = [t[0].size for t in turned]
    both = jnp.concatenate([t.reshape(-1, w) for t, w in zip(turned, widths)], axis=1)
    whole = lax.all_gather(both, axis, axis=0, tiled=True)
    blocks = jnp.split(whole, [sum(widths[:k]) for k in range(1, len(widths))], axis=1)
    return tuple(
        (
            jnp.moveaxis(b.reshape(-1, *t.shape[1:]), 0, dim)
            for b, t, dim in zip(blocks, turned, dims)
        )
    )


def from_behind(x, axis, by):
    size = lax.axis_size(axis)
    return lax.ppermute(x, axis, [(i, (i + by) % size) for i in range(size)])


def passed_along(block, axis, distance):
    devices = range(lax.axis_size(axis))
    route = [(i - distance, i) for i in devices if i - distance in devices]
    return lax.ppermute(block, axis, route)


def normed_rows(expanded_rows):
    scale = lax.rsqrt(jnp.mean(expanded_rows * expanded_rows, axis=-1, keepdims=True) + EPSILON)
    return (expanded_rows * scale).astype(jnp.bfloat16)


def encoder_act(values):
    return jax.nn.gelu(values, approximate=False)


def adapter_layer(hidden, weight_in, weight_out, nonlinear):
    expanded_rows = hidden.astype(jnp.float32)
    normed = normed_rows(expanded_rows)
    projected = jnp.dot(normed, weight_in, preferred_element_type=jnp.float32)
    activated = nonlinear(projected).astype(jnp.bfloat16)
    branch = jnp.dot(activated, weight_out, preferred_element_type=jnp.float32)
    return (expanded_rows + branch).astype(jnp.bfloat16)


def first_factor(encoded, weight_in):
    projected = jnp.dot(
        normed_rows(encoded.astype(jnp.float32)), weight_in, preferred_element_type=jnp.float32
    )
    return encoder_act(projected).astype(jnp.bfloat16)


def evaluate_model(tick_index, incoming, finished, pieces_in, layer_fn, section_index):
    item_count = pieces_in.shape[0]
    position = tick_index - section_index
    slot_index = jnp.clip(position, 0, item_count - 1)
    source = jnp.where(
        section_index == 0,
        lax.dynamic_index_in_dim(pieces_in, slot_index, 0, keepdims=False),
        incoming,
    )
    result = layer_fn(source)
    is_valid = (position >= 0) & (position < item_count)
    current = lax.dynamic_index_in_dim(finished, slot_index, 0, keepdims=False)
    chosen = jnp.where(is_valid, result, current)
    finished = lax.dynamic_update_index_in_dim(finished, chosen, slot_index, 0)
    return (result, finished)


def run_sections(pieces_in, layer_fn, send_fn, section_index, section_count):
    item_count = pieces_in.shape[0]
    tick_count = item_count + section_count - 1

    def advance(tick_index, carry):
        incoming, finished = carry
        result, finished = evaluate_model(
            tick_index, incoming, finished, pieces_in, layer_fn, section_index
        )
        return (send_fn(result), finished)

    initial = (jnp.zeros_like(pieces_in[0]), jnp.zeros_like(pieces_in))
    incoming, finished = lax.fori_loop(0, tick_count - 1, advance, initial)
    unused, finished = evaluate_model(
        tick_count - 1, incoming, finished, pieces_in, layer_fn, section_index
    )
    return finished


def run_encoder_loop(pieces_in, layer_fn, send_fn, section_index, section_count):
    item_count = pieces_in.shape[0]
    tick_count = item_count + section_count - 1

    def advance(tick_index, carry):
        incoming, finished, collected = carry
        result, finished = evaluate_model(
            tick_index, incoming, finished, pieces_in, layer_fn, section_index
        )
        received = send_fn(result)
        item_index = tick_index - (section_count - 1)
        slot_index = jnp.clip(item_index, 0, item_count - 1)
        is_valid = (item_index >= 0) & (item_index < item_count)
        current = lax.dynamic_index_in_dim(collected, slot_index, 0, keepdims=False)
        chosen = jnp.where(is_valid, received, current)
        collected = lax.dynamic_update_index_in_dim(collected, chosen, slot_index, 0)
        return (received, finished, collected)

    initial = (jnp.zeros_like(pieces_in[0]), jnp.zeros_like(pieces_in), jnp.zeros_like(pieces_in))
    incoming, finished, collected = lax.fori_loop(0, tick_count, advance, initial)
    return collected


def local(text, image, positions, enc_in, enc_out, conn_in, conn_out, llm_in, llm_out):
    section_index = lax.axis_index("section")
    section_count = lax.axis_size("section")
    encoder_down, encoder_up = (gathered_copies(enc_in, "dp", 1), gathered_copies(enc_out, "dp", 2))
    joint_down, joint_up = (gathered_copies(conn_in, "dp", 0), gathered_copies(conn_out, "dp", 1))
    decoder_down, decoder_up = rows_first((llm_in, llm_out), "dp", (1, 2))
    micro_count = positions.shape[0]
    image_count = positions.shape[1]
    row_count = text.shape[0] // micro_count
    model_width = text.shape[1]
    vision_width = image.shape[1]
    encoder_items = image.reshape(micro_count, image_count, vision_width)
    features = run_encoder_loop(
        encoder_items,
        lambda hidden: adapter_layer(hidden, encoder_down[0], encoder_up[0], encoder_act),
        lambda result: from_behind(result, "section", 1),
        section_index,
        section_count,
    )
    latent = first_factor(features.reshape(micro_count * image_count, vision_width), joint_down)
    picture_row_block = jnp.dot(latent, joint_up, preferred_element_type=jnp.float32).astype(
        jnp.bfloat16
    )
    picture_row_block = picture_row_block.reshape(micro_count, image_count, model_width)
    row_ids = lax.broadcasted_iota(jnp.int32, (1, 1, row_count), 2)
    matches = positions[:, :, None] == row_ids
    indicator_vector = matches.astype(jnp.bfloat16)
    placed = jnp.einsum(
        "nsq,nsc->nqc", indicator_vector, picture_row_block, preferred_element_type=jnp.float32
    ).astype(jnp.bfloat16)
    is_image = jnp.any(matches, axis=1)
    first_state = jnp.where(
        is_image[:, :, None], placed, text.reshape(micro_count, row_count, model_width)
    )
    piece_count = 2
    decoder_items = first_state.reshape(
        micro_count * piece_count, row_count // piece_count, model_width
    )
    hidden_state_list = run_sections(
        decoder_items,
        lambda hidden: adapter_layer(hidden, decoder_down[0], decoder_up[0], jax.nn.silu),
        lambda result: passed_along(result, "section", 1),
        section_index,
        section_count,
    )
    return hidden_state_list.reshape(1, micro_count * row_count, model_width)


def solution(mesh):
    return jax.shard_map(
        local,
        mesh=mesh,
        in_specs=(
            P("dp", None),
            P("dp", None),
            P("dp", None),
            P("section", "dp", None),
            P("section", None, "dp"),
            P("dp", None),
            P(None, "dp"),
            P("section", "dp", None),
            P("section", None, "dp"),
        ),
        out_specs=P("section", "dp", None),
        check_vma=False,
    )
```

profile of v0, /device:TPU:44, one launch (start us, length us, event | category | flops | bytes accessed | tf_op | source)
XLA Modules:
  0.0 781.7 jit_solution(13487611671383648761)
XLA Ops:
  10.3 25.0 %all_to_all.20 = bf16[32,100,64]{1,2,0:T(8,128)(2,1)S(1)} all-to-all(bf16[32,100,64]{1,2,0:T(8,128)(2,1)S(1)} %broadcast_in_dim.72), channel_id=1, replica_groups=mesh['section'=8,'dp'=32] {'dp'}, dimensions={0} | all-to-all | bytes 819200 | tf_op jit(solution)/shard_map/all_to_all | solution.py:11
  35.4 35.6 %all_to_all.21 = bf16[32,1,128,100]{2,3,1,0:T(8,128)(2,1)S(1)} all-to-all(bf16[32,1,128,100]{2,3,1,0:T(8,128)(2,1)S(1)} %broadcast_in_dim.71), channel_id=1, replica_groups=mesh['section'=8,'dp'=32] {'dp'}, dimensions={0} | all-to-all | bytes 1638400 | tf_op jit(solution)/shard_map/all_to_all | solution.py:11
  81.8 26.1 %all-to-all-done = bf16[32,1,100,128]{3,2,1,0:T(8,128)(2,1)S(1)} async-done(((bf16[32,1,100,128]{3,2,1,0:T(8,128)(2,1)}), bf16[32,1,100,128]{3,2,1,0:T(8,128)(2,1)S(1)}, u32[]{:S(2)}, u32[]{:S(2)}) %all-to-all-start) | async-done | bytes 819232 | tf_op jit(solution)/shard_map/all_to_all | solution.py:11
  118.2 120.7 %while.35 = (s32[]{:T(128)}, bf16[16,3200]{1,0:T(8,128)(2,1)S(1)}, bf16[3,16,3200]{2,1,0:T(8,128)(2,1)S(1)}, pred[]{:T(512)}, s32[]{:T(128)}, /*index=5*/bf16[3,...) while((s32[]{:T(128)}, bf16[16,3200]{1,0:T(8,128)(2,1)S(1)}, ...), condition=%wide.wide.region_3.4_spmd, body=%wide.wide.region_1.3_spmd.sunk | while | flops 27013140 | bytes 3279392 | solution.py:130
  124.3 10.1 %collective-permute-done.1 = bf16[16,3200]{1,0:T(8,128)(2,1)S(1)} collective-permute-done((bf16[16,3200]{1,0:T(8,128)(2,1)}, bf16[16,3200]{1,0:T(8,128)(2,1)S(1)}, u32[]{:S(2)}, u32[]{:S(2)}) %collective-permute-start.1) | collective-permute-done | bytes 102432 | tf_op jit(solution)/shard_map/while/body/eval_jaxpr/ppermute | solution.py:41
  245.9 11.6 %slice_bitcast_fusion = (bf16[1,512,8192]{2,1,0:T(8,128)(2,1)}, bf16[8192,512]{0,1:T(8,128)(2,1)}) fusion(bf16[8192,1024]{0,1:T(8,128)(2,1)} %all-gather.2.cloned.1.call-done), kind=kLoop, calls=%fused_computation.121 | loop fusion | bytes 33554432 | tf_op jit(solution)/shard_map/transpose | solution.py:33
  257.5 11.9 %copy.21 = bf16[8192,512]{1,0:T(8,128)(2,1)} copy(bf16[8192,512]{0,1:T(8,128)(2,1)} %get-tuple-element.415) | data formatting | bytes 16777216 | tf_op jit(solution)/shard_map/while | solution.py:104
  271.5 490.0 %while.34 = (s32[]{:T(128)}, bf16[32,8192]{1,0:T(8,128)(2,1)S(1)}, bf16[6,32,8192]{2,1,0:T(8,128)(2,1)}, pred[]{:T(512)}, s32[]{:T(128)}, /*index=5*/bf16[6,32,8...) while((s32[]{:T(128)}, bf16[32,8192]{1,0:T(8,128)(2,1)S(1)}, ...), condition=%wide.region_7.8_spmd, body=%wide.region_5.7_spmd.sunk | while | flops 540360768 | bytes 24645216 | solution.py:104
  292.7 14.2 %collective-permute-done = bf16[32,8192]{1,0:T(8,128)(2,1)S(1)} collective-permute-done((bf16[32,8192]{1,0:T(8,128)(2,1)S(1)}, bf16[32,8192]{1,0:T(8,128)(2,1)S(1)}, u32[]{:S(2)}, u32[]{:S(2)}) %collective-permute-start) | collective-permute-done | bytes 524320 | tf_op jit(solution)/shard_map/while/body/eval_jaxpr/ppermute | solution.py:47
  309.3 9.9 %bitcast_dynamic-update-slice_fusion.5 = (bf16[6,32,8192]{2,1,0:T(8,128)(2,1)}, bf16[32,8192]{1,0:T(8,128)(2,1)S(1)}) fusion(bf16[6,32,8192]{2,1,0:T(8,128)(2,1)} %get-tuple-element.620, s32[]{:T(128)S(6)} %min.39, bf16[1,32,8192]{2,1,0:T(8,128)(2,1)S(1)} %constant_dynamic-slice_fusion.6, pred[]{:T(512)S(6)} %and.26, ...), kind=kOutput, calls=%fused_computation.101.clone.1 | convolution fusion | flops 539312128 | bytes 20450304 | tf_op jit(solution)/shard_map/while/body/eval_jaxpr/dot_general | solution.py:64
  327.1 21.2 %collective-permute-done = bf16[32,8192]{1,0:T(8,128)(2,1)S(1)} collective-permute-done((bf16[32,8192]{1,0:T(8,128)(2,1)S(1)}, bf16[32,8192]{1,0:T(8,128)(2,1)S(1)}, u32[]{:S(2)}, u32[]{:S(2)}) %collective-permute-start) | collective-permute-done | bytes 524320 | tf_op jit(solution)/shard_map/while/body/eval_jaxpr/ppermute | solution.py:47
  350.7 9.9 %bitcast_dynamic-update-slice_fusion.5 = (bf16[6,32,8192]{2,1,0:T(8,128)(2,1)}, bf16[32,8192]{1,0:T(8,128)(2,1)S(1)}) fusion(bf16[6,32,8192]{2,1,0:T(8,128)(2,1)} %get-tuple-element.620, s32[]{:T(128)S(6)} %min.39, bf16[1,32,8192]{2,1,0:T(8,128)(2,1)S(1)} %constant_dynamic-slice_fusion.6, pred[]{:T(512)S(6)} %and.26, ...), kind=kOutput, calls=%fused_computation.101.clone.1 | convolution fusion | flops 539312128 | bytes 20450304 | tf_op jit(solution)/shard_map/while/body/eval_jaxpr/dot_general | solution.py:64
  360.7 21.5 %collective-permute-start = (bf16[32,8192]{1,0:T(8,128)(2,1)S(1)}, bf16[32,8192]{1,0:T(8,128)(2,1)S(1)}, u32[]{:S(2)}, u32[]{:S(2)}) collective-permute-start(bf16[32,8192]{1,0:T(8,128)(2,1)S(1)} %get-tuple-element.549), channel_id=1, source_target_pairs={{0,32},{32,64},{64,96},{96,128},{128,160},{160,192},{192,224},{1,3... | collective-permute-start | bytes 1572872 | tf_op jit(solution)/shard_map/while/body/eval_jaxpr/ppermute | solution.py:47
  382.1 18.2 %collective-permute-done = bf16[32,8192]{1,0:T(8,128)(2,1)S(1)} collective-permute-done((bf16[32,8192]{1,0:T(8,128)(2,1)S(1)}, bf16[32,8192]{1,0:T(8,128)(2,1)S(1)}, u32[]{:S(2)}, u32[]{:S(2)}) %collective-permute-start) | collective-permute-done | bytes 524320 | tf_op jit(solution)/shard_map/while/body/eval_jaxpr/ppermute | solution.py:47
  421.0 23.6 %collective-permute-done = bf16[32,8192]{1,0:T(8,128)(2,1)S(1)} collective-permute-done((bf16[32,8192]{1,0:T(8,128)(2,1)S(1)}, bf16[32,8192]{1,0:T(8,128)(2,1)S(1)}, u32[]{:S(2)}, u32[]{:S(2)}) %collective-permute-start) | collective-permute-done | bytes 524320 | tf_op jit(solution)/shard_map/while/body/eval_jaxpr/ppermute | solution.py:47
  458.9 28.9 %collective-permute-done = bf16[32,8192]{1,0:T(8,128)(2,1)S(1)} collective-permute-done((bf16[32,8192]{1,0:T(8,128)(2,1)S(1)}, bf16[32,8192]{1,0:T(8,128)(2,1)S(1)}, u32[]{:S(2)}, u32[]{:S(2)}) %collective-permute-start) | collective-permute-done | bytes 524320 | tf_op jit(solution)/shard_map/while/body/eval_jaxpr/ppermute | solution.py:47
  502.1 24.3 %collective-permute-done = bf16[32,8192]{1,0:T(8,128)(2,1)S(1)} collective-permute-done((bf16[32,8192]{1,0:T(8,128)(2,1)S(1)}, bf16[32,8192]{1,0:T(8,128)(2,1)S(1)}, u32[]{:S(2)}, u32[]{:S(2)}) %collective-permute-start) | collective-permute-done | bytes 524320 | tf_op jit(solution)/shard_map/while/body/eval_jaxpr/ppermute | solution.py:47
  540.7 27.0 %collective-permute-done = bf16[32,8192]{1,0:T(8,128)(2,1)S(1)} collective-permute-done((bf16[32,8192]{1,0:T(8,128)(2,1)S(1)}, bf16[32,8192]{1,0:T(8,128)(2,1)S(1)}, u32[]{:S(2)}, u32[]{:S(2)}) %collective-permute-start) | collective-permute-done | bytes 524320 | tf_op jit(solution)/shard_map/while/body/eval_jaxpr/ppermute | solution.py:47
  581.9 21.8 %collective-permute-done = bf16[32,8192]{1,0:T(8,128)(2,1)S(1)} collective-permute-done((bf16[32,8192]{1,0:T(8,128)(2,1)S(1)}, bf16[32,8192]{1,0:T(8,128)(2,1)S(1)}, u32[]{:S(2)}, u32[]{:S(2)}) %collective-permute-start) | collective-permute-done | bytes 524320 | tf_op jit(solution)/shard_map/while/body/eval_jaxpr/ppermute | solution.py:47
  624.4 15.0 %collective-permute-done = bf16[32,8192]{1,0:T(8,128)(2,1)S(1)} collective-permute-done((bf16[32,8192]{1,0:T(8,128)(2,1)S(1)}, bf16[32,8192]{1,0:T(8,128)(2,1)S(1)}, u32[]{:S(2)}, u32[]{:S(2)}) %collective-permute-start) | collective-permute-done | bytes 524320 | tf_op jit(solution)/shard_map/while/body/eval_jaxpr/ppermute | solution.py:47
  660.1 18.5 %collective-permute-done = bf16[32,8192]{1,0:T(8,128)(2,1)S(1)} collective-permute-done((bf16[32,8192]{1,0:T(8,128)(2,1)S(1)}, bf16[32,8192]{1,0:T(8,128)(2,1)S(1)}, u32[]{:S(2)}, u32[]{:S(2)}) %collective-permute-start) | collective-permute-done | bytes 524320 | tf_op jit(solution)/shard_map/while/body/eval_jaxpr/ppermute | solution.py:47
  699.5 22.5 %collective-permute-done = bf16[32,8192]{1,0:T(8,128)(2,1)S(1)} collective-permute-done((bf16[32,8192]{1,0:T(8,128)(2,1)S(1)}, bf16[32,8192]{1,0:T(8,128)(2,1)S(1)}, u32[]{:S(2)}, u32[]{:S(2)}) %collective-permute-start) | collective-permute-done | bytes 524320 | tf_op jit(solution)/shard_map/while/body/eval_jaxpr/ppermute | solution.py:47
  742.7 18.8 %collective-permute-done = bf16[32,8192]{1,0:T(8,128)(2,1)S(1)} collective-permute-done((bf16[32,8192]{1,0:T(8,128)(2,1)S(1)}, bf16[32,8192]{1,0:T(8,128)(2,1)S(1)}, u32[]{:S(2)}, u32[]{:S(2)}) %collective-permute-start) | collective-permute-done | bytes 524320 | tf_op jit(solution)/shard_map/while/body/eval_jaxpr/ppermute | solution.py:47
  763.9 10.9 %fusion.101 = bf16[6,32,8192]{2,1,0:T(8,128)(2,1)} fusion(bf16[6,32,8192]{2,1,0:T(8,128)(2,1)} %get-tuple-element.346, s32[]{:T(128)S(6)} %min.33, bf16[8192,1024]{0,1:T(8,128)(2,1)} %all-gather.2.cloned.1.call-done, bf16[1,32,8192]{2,1,0:T(8,128)(2,1)S(1)} %constant_dynamic-slice_fusion.2, pred[]{:T(512)S(6)} %and.22, f32[32]{0:T(128)S(1)} %add_rsqrt_fusion.3, ...), kind=kOutput, calls=%fused_computation.118 | convolution fusion | flops 539312128 | bytes 19926016 | tf_op jit(solution)/shard_map/dot_general | solution.py:64
  (170 shorter events, 340.8 us)
Async XLA Ops:
  6.5 239.3 %all-gather.2.cloned.1.call-start = ((), (), s32[]{:S(2)}) async-start(), calls=%async_computation.4 | async-start | bytes 17301504 | tf_op jit(solution)/shard_map/all_gather | solution.py:29
  72.2 35.7 %all-to-all-start = ((bf16[32,1,100,128]{3,2,1,0:T(8,128)(2,1)}), bf16[32,1,100,128]{3,2,1,0:T(8,128)(2,1)S(1)}, u32[]{:S(2)}, u32[]{:S(2)}) async-start(bf16[32,1,100,128]{3,2,1,0:T(8,128)(2,1)} %broadcast_in_dim.70), calls=%async_computation | async-start | bytes 1703936 | tf_op jit(solution)/shard_map/all_to_all | solution.py:11
  109.1 130.1 %all-to-all-start.3 = ((bf16[32,64,256]{2,1,0:T(8,128)(2,1)}), bf16[32,64,256]{2,1,0:T(8,128)(2,1)S(1)}, u32[]{:S(2)}, u32[]{:S(2)}) async-start(bf16[32,64,256]{2,1,0:T(8,128)(2,1)} %broadcast_in_dim.73), calls=%async_computation.3 | async-start | bytes 2097152 | tf_op jit(solution)/shard_map/all_to_all | solution.py:11
  119.7 14.7 %collective-permute-start.1 = (bf16[16,3200]{1,0:T(8,128)(2,1)}, bf16[16,3200]{1,0:T(8,128)(2,1)S(1)}, u32[]{:S(2)}, u32[]{:S(2)}) collective-permute-start(bf16[16,3200]{1,0:T(8,128)(2,1)} %fusion.225), channel_id=1, source_target_pairs={{0,32},{32,64},{64,96},{96,128},{128,160},{160,192},{192,224},{224... | collective-permute-start | bytes 307208 | tf_op jit(solution)/shard_map/while/body/eval_jaxpr/ppermute | solution.py:41
  135.9 11.6 %collective-permute-start.1 = (bf16[16,3200]{1,0:T(8,128)(2,1)}, bf16[16,3200]{1,0:T(8,128)(2,1)S(1)}, u32[]{:S(2)}, u32[]{:S(2)}) collective-permute-start(bf16[16,3200]{1,0:T(8,128)(2,1)} %fusion.225), channel_id=1, source_target_pairs={{0,32},{32,64},{64,96},{96,128},{128,160},{160,192},{192,224},{224... | collective-permute-start | bytes 307208 | tf_op jit(solution)/shard_map/while/body/eval_jaxpr/ppermute | solution.py:41
  149.0 10.5 %collective-permute-start.1 = (bf16[16,3200]{1,0:T(8,128)(2,1)}, bf16[16,3200]{1,0:T(8,128)(2,1)S(1)}, u32[]{:S(2)}, u32[]{:S(2)}) collective-permute-start(bf16[16,3200]{1,0:T(8,128)(2,1)} %fusion.225), channel_id=1, source_target_pairs={{0,32},{32,64},{64,96},{96,128},{128,160},{160,192},{192,224},{224... | collective-permute-start | bytes 307208 | tf_op jit(solution)/shard_map/while/body/eval_jaxpr/ppermute | solution.py:41
  161.0 10.3 %collective-permute-start.1 = (bf16[16,3200]{1,0:T(8,128)(2,1)}, bf16[16,3200]{1,0:T(8,128)(2,1)S(1)}, u32[]{:S(2)}, u32[]{:S(2)}) collective-permute-start(bf16[16,3200]{1,0:T(8,128)(2,1)} %fusion.225), channel_id=1, source_target_pairs={{0,32},{32,64},{64,96},{96,128},{128,160},{160,192},{192,224},{224... | collective-permute-start | bytes 307208 | tf_op jit(solution)/shard_map/while/body/eval_jaxpr/ppermute | solution.py:41
  172.9 9.8 %collective-permute-start.1 = (bf16[16,3200]{1,0:T(8,128)(2,1)}, bf16[16,3200]{1,0:T(8,128)(2,1)S(1)}, u32[]{:S(2)}, u32[]{:S(2)}) collective-permute-start(bf16[16,3200]{1,0:T(8,128)(2,1)} %fusion.225), channel_id=1, source_target_pairs={{0,32},{32,64},{64,96},{96,128},{128,160},{160,192},{192,224},{224... | collective-permute-start | bytes 307208 | tf_op jit(solution)/shard_map/while/body/eval_jaxpr/ppermute | solution.py:41
  184.2 9.8 %collective-permute-start.1 = (bf16[16,3200]{1,0:T(8,128)(2,1)}, bf16[16,3200]{1,0:T(8,128)(2,1)S(1)}, u32[]{:S(2)}, u32[]{:S(2)}) collective-permute-start(bf16[16,3200]{1,0:T(8,128)(2,1)} %fusion.225), channel_id=1, source_target_pairs={{0,32},{32,64},{64,96},{96,128},{128,160},{160,192},{192,224},{224... | collective-permute-start | bytes 307208 | tf_op jit(solution)/shard_map/while/body/eval_jaxpr/ppermute | solution.py:41
  195.5 9.8 %collective-permute-start.1 = (bf16[16,3200]{1,0:T(8,128)(2,1)}, bf16[16,3200]{1,0:T(8,128)(2,1)S(1)}, u32[]{:S(2)}, u32[]{:S(2)}) collective-permute-start(bf16[16,3200]{1,0:T(8,128)(2,1)} %fusion.225), channel_id=1, source_target_pairs={{0,32},{32,64},{64,96},{96,128},{128,160},{160,192},{192,224},{224... | collective-permute-start | bytes 307208 | tf_op jit(solution)/shard_map/while/body/eval_jaxpr/ppermute | solution.py:41
  206.8 9.7 %collective-permute-start.1 = (bf16[16,3200]{1,0:T(8,128)(2,1)}, bf16[16,3200]{1,0:T(8,128)(2,1)S(1)}, u32[]{:S(2)}, u32[]{:S(2)}) collective-permute-start(bf16[16,3200]{1,0:T(8,128)(2,1)} %fusion.225), channel_id=1, source_target_pairs={{0,32},{32,64},{64,96},{96,128},{128,160},{160,192},{192,224},{224... | collective-permute-start | bytes 307208 | tf_op jit(solution)/shard_map/while/body/eval_jaxpr/ppermute | solution.py:41
  229.2 9.8 %collective-permute-start.1 = (bf16[16,3200]{1,0:T(8,128)(2,1)}, bf16[16,3200]{1,0:T(8,128)(2,1)S(1)}, u32[]{:S(2)}, u32[]{:S(2)}) collective-permute-start(bf16[16,3200]{1,0:T(8,128)(2,1)} %fusion.225), channel_id=1, source_target_pairs={{0,32},{32,64},{64,96},{96,128},{128,160},{160,192},{192,224},{224... | collective-permute-start | bytes 307208 | tf_op jit(solution)/shard_map/while/body/eval_jaxpr/ppermute | solution.py:41
  283.9 23.0 %collective-permute-start = (bf16[32,8192]{1,0:T(8,128)(2,1)S(1)}, bf16[32,8192]{1,0:T(8,128)(2,1)S(1)}, u32[]{:S(2)}, u32[]{:S(2)}) collective-permute-start(bf16[32,8192]{1,0:T(8,128)(2,1)S(1)} %get-tuple-element.549), channel_id=1, source_target_pairs={{0,32},{32,64},{64,96},{96,128},{128,160},{160,192},{192,224},{1,3... | collective-permute-start | bytes 1572872 | tf_op jit(solution)/shard_map/while/body/eval_jaxpr/ppermute | solution.py:47
  319.2 29.1 %collective-permute-start = (bf16[32,8192]{1,0:T(8,128)(2,1)S(1)}, bf16[32,8192]{1,0:T(8,128)(2,1)S(1)}, u32[]{:S(2)}, u32[]{:S(2)}) collective-permute-start(bf16[32,8192]{1,0:T(8,128)(2,1)S(1)} %get-tuple-element.549), channel_id=1, source_target_pairs={{0,32},{32,64},{64,96},{96,128},{128,160},{160,192},{192,224},{1,3... | collective-permute-start | bytes 1572872 | tf_op jit(solution)/shard_map/while/body/eval_jaxpr/ppermute | solution.py:47
  360.7 39.6 %collective-permute-start = (bf16[32,8192]{1,0:T(8,128)(2,1)S(1)}, bf16[32,8192]{1,0:T(8,128)(2,1)S(1)}, u32[]{:S(2)}, u32[]{:S(2)}) collective-permute-start(bf16[32,8192]{1,0:T(8,128)(2,1)S(1)} %get-tuple-element.549), channel_id=1, source_target_pairs={{0,32},{32,64},{64,96},{96,128},{128,160},{160,192},{192,224},{1,3... | collective-permute-start | bytes 1572872 | tf_op jit(solution)/shard_map/while/body/eval_jaxpr/ppermute | solution.py:47
  412.7 31.9 %collective-permute-start = (bf16[32,8192]{1,0:T(8,128)(2,1)S(1)}, bf16[32,8192]{1,0:T(8,128)(2,1)S(1)}, u32[]{:S(2)}, u32[]{:S(2)}) collective-permute-start(bf16[32,8192]{1,0:T(8,128)(2,1)S(1)} %get-tuple-element.549), channel_id=1, source_target_pairs={{0,32},{32,64},{64,96},{96,128},{128,160},{160,192},{192,224},{1,3... | collective-permute-start | bytes 1572872 | tf_op jit(solution)/shard_map/while/body/eval_jaxpr/ppermute | solution.py:47
  456.9 30.9 %collective-permute-start = (bf16[32,8192]{1,0:T(8,128)(2,1)S(1)}, bf16[32,8192]{1,0:T(8,128)(2,1)S(1)}, u32[]{:S(2)}, u32[]{:S(2)}) collective-permute-start(bf16[32,8192]{1,0:T(8,128)(2,1)S(1)} %get-tuple-element.549), channel_id=1, source_target_pairs={{0,32},{32,64},{64,96},{96,128},{128,160},{160,192},{192,224},{1,3... | collective-permute-start | bytes 1572872 | tf_op jit(solution)/shard_map/while/body/eval_jaxpr/ppermute | solution.py:47
  500.2 26.2 %collective-permute-start = (bf16[32,8192]{1,0:T(8,128)(2,1)S(1)}, bf16[32,8192]{1,0:T(8,128)(2,1)S(1)}, u32[]{:S(2)}, u32[]{:S(2)}) collective-permute-start(bf16[32,8192]{1,0:T(8,128)(2,1)S(1)} %get-tuple-element.549), channel_id=1, source_target_pairs={{0,32},{32,64},{64,96},{96,128},{128,160},{160,192},{192,224},{1,3... | collective-permute-start | bytes 1572872 | tf_op jit(solution)/shard_map/while/body/eval_jaxpr/ppermute | solution.py:47
  538.8 28.9 %collective-permute-start = (bf16[32,8192]{1,0:T(8,128)(2,1)S(1)}, bf16[32,8192]{1,0:T(8,128)(2,1)S(1)}, u32[]{:S(2)}, u32[]{:S(2)}) collective-permute-start(bf16[32,8192]{1,0:T(8,128)(2,1)S(1)} %get-tuple-element.549), channel_id=1, source_target_pairs={{0,32},{32,64},{64,96},{96,128},{128,160},{160,192},{192,224},{1,3... | collective-permute-start | bytes 1572872 | tf_op jit(solution)/shard_map/while/body/eval_jaxpr/ppermute | solution.py:47
  580.0 23.7 %collective-permute-start = (bf16[32,8192]{1,0:T(8,128)(2,1)S(1)}, bf16[32,8192]{1,0:T(8,128)(2,1)S(1)}, u32[]{:S(2)}, u32[]{:S(2)}) collective-permute-start(bf16[32,8192]{1,0:T(8,128)(2,1)S(1)} %get-tuple-element.549), channel_id=1, source_target_pairs={{0,32},{32,64},{64,96},{96,128},{128,160},{160,192},{192,224},{1,3... | collective-permute-start | bytes 1572872 | tf_op jit(solution)/shard_map/while/body/eval_jaxpr/ppermute | solution.py:47
  616.1 23.3 %collective-permute-start = (bf16[32,8192]{1,0:T(8,128)(2,1)S(1)}, bf16[32,8192]{1,0:T(8,128)(2,1)S(1)}, u32[]{:S(2)}, u32[]{:S(2)}) collective-permute-start(bf16[32,8192]{1,0:T(8,128)(2,1)S(1)} %get-tuple-element.549), channel_id=1, source_target_pairs={{0,32},{32,64},{64,96},{96,128},{128,160},{160,192},{192,224},{1,3... | collective-permute-start | bytes 1572872 | tf_op jit(solution)/shard_map/while/body/eval_jaxpr/ppermute | solution.py:47
  651.8 26.8 %collective-permute-start = (bf16[32,8192]{1,0:T(8,128)(2,1)S(1)}, bf16[32,8192]{1,0:T(8,128)(2,1)S(1)}, u32[]{:S(2)}, u32[]{:S(2)}) collective-permute-start(bf16[32,8192]{1,0:T(8,128)(2,1)S(1)} %get-tuple-element.549), channel_id=1, source_target_pairs={{0,32},{32,64},{64,96},{96,128},{128,160},{160,192},{192,224},{1,3... | collective-permute-start | bytes 1572872 | tf_op jit(solution)/shard_map/while/body/eval_jaxpr/ppermute | solution.py:47
  691.0 31.0 %collective-permute-start = (bf16[32,8192]{1,0:T(8,128)(2,1)S(1)}, bf16[32,8192]{1,0:T(8,128)(2,1)S(1)}, u32[]{:S(2)}, u32[]{:S(2)}) collective-permute-start(bf16[32,8192]{1,0:T(8,128)(2,1)S(1)} %get-tuple-element.549), channel_id=1, source_target_pairs={{0,32},{32,64},{64,96},{96,128},{128,160},{160,192},{192,224},{1,3... | collective-permute-start | bytes 1572872 | tf_op jit(solution)/shard_map/while/body/eval_jaxpr/ppermute | solution.py:47
  734.4 27.1 %collective-permute-start = (bf16[32,8192]{1,0:T(8,128)(2,1)S(1)}, bf16[32,8192]{1,0:T(8,128)(2,1)S(1)}, u32[]{:S(2)}, u32[]{:S(2)}) collective-permute-start(bf16[32,8192]{1,0:T(8,128)(2,1)S(1)} %get-tuple-element.549), channel_id=1, source_target_pairs={{0,32},{32,64},{64,96},{96,128},{128,160},{160,192},{192,224},{1,3... | collective-permute-start | bytes 1572872 | tf_op jit(solution)/shard_map/while/body/eval_jaxpr/ppermute | solution.py:47
  (8 other events, 285.1 us)
Sparse Core Ops, SparseCore 0:
  9.6 199.9 all-gather.1
where the time goes:
time: 784 us; the launch traced here: 782 us
  waiting for transfers between devices  365 us (47%)
  matrix products  150 us (19%)
  starting transfers between devices  123 us (16%)
  blocking collectives  60.6 us (8%)
  local copies, waits for them, and re-layouts  47.6 us (6%)
  other arithmetic  21.4 us (3%)
  between operations  13.5 us (2%)
    ppermute x12, waiting for transfers between devices, passed_along(): return lax.ppermute(block, axis, route)  254 us
    dot_general x23, matrix products, adapter_layer(): branch = jnp.dot(activated, weight_out, preferred_element_type=jnp.float32)  143 us
    ppermute x12, starting transfers between devices, passed_along(): return lax.ppermute(block, axis, route)  87.5 us
    ppermute x10, waiting for transfers between devices, from_behind(): return lax.ppermute(x, axis, [(i, (i + by) % size) for i in range(size)])  85.3 us
    all_to_all x2, blocking collectives, copy_for_each(): return lax.all_to_all(copies, axis, split_axis=0, concat_axis=0, tiled=True)  60.6 us
    all_to_all x2, waiting for transfers between devices, copy_for_each(): return lax.all_to_all(copies, axis, split_axis=0, concat_axis=0, tiled=True)  26.1 us
    ppermute x10, starting transfers between devices, from_behind(): return lax.ppermute(x, axis, [(i, (i + by) % size) for i in range(size)])  20 us
    reduce_sum x24, other arithmetic, normed_rows(): jnp.mean(expanded_rows * expanded_rows, axis=-1, keepdims=True) + EPSILON  18.8 us
  transfers between devices with their start and end apart: 25, of which 23 were waited for; matrix products, arithmetic and copies ran while one was open for 4% of the time, Pallas kernels for 0%

commit v1 on v0

v1 whole, which is shorter than its diff:
```python
import jax
import jax.numpy as jnp
from jax import lax
from jax.experimental import pallas as pl
from jax.experimental.pallas import tpu as pltpu
from jax.sharding import PartitionSpec as P

EPSILON = 1e-06
MESH = pl.DeviceIdType.MESH
F32 = jnp.float32
BF16 = jnp.bfloat16
CHUNKS = 6
BLOCKS = 16


def gelu(v):
    return 0.5 * v * (1.0 + lax.erf(v * 0.7071067811865476))


def silu(v):
    return v / (1.0 + jnp.exp(-v))


def matmul(a, b):
    return jnp.dot(a, b, preferred_element_type=F32)


def device(x, y, z, c):
    return (x * 2 + z // 4, lax.rem(z, 4) * 8 + y * 2 + c)


def kernel(
    text, wa, wb, e3, img, oh, out,
    A, B, E1, E2, h0, ohb, henc, lat, latr, imgrows, xs, xr, es, er, hin, osend, orecv,
    send, recv_llm, recv_enc, own_sem, gather_s, gather_r, text_l, text_s, text_r,
    misc_s, misc_r, x_s, x_r, xe_s, xe_r, flow_s, flow_r, out_s, out_r,
):
    section = lax.axis_index("section")
    dp = lax.axis_index("dp")
    x, z_hi = section // 2, lax.rem(section, 2)
    z = z_hi * 4 + dp // 8
    y = lax.rem(dp // 2, 4)
    c = lax.rem(dp, 2)
    o = 1 - c
    me = z * 4 + y

    def up(v, by, n):
        return lax.rem(v + by + n, n)

    y_up, y_down = device(x, up(y, 1, 4), z, c), device(x, up(y, -1, 4), z, c)
    z_up, z_down = device(x, y, up(z, 1, 8), c), device(x, y, up(z, -1, 8), c)
    other = device(x, y, z, o)
    x_next = device(up(x, 1, 4), y, z, c)
    plane3, plane0 = device(3, y, z, c), device(0, y, z, c)

    def remote(src, dst, ssem, rsem, to):
        return pltpu.make_async_remote_copy(
            src_ref=src, dst_ref=dst, send_sem=ssem, recv_sem=rsem, device_id=to, device_id_type=MESH
        )

    own = [
        pltpu.make_async_copy(wa, A.at[me], own_sem.at[0]),
        pltpu.make_async_copy(wb, B.at[me], own_sem.at[1]),
    ]
    for copy in own:
        copy.start()

    barrier = pltpu.get_barrier_semaphore()
    for to in (
        y_up, y_down, z_up, z_down, other, x_next,
        device(up(x, 2, 4), y, z, c), device(up(x, 3, 4), y, z, c),
    ):
        pl.semaphore_signal(barrier, inc=1, device_id=to, device_id_type=MESH)
    pl.semaphore_wait(barrier, 8)

    def to_plane3(k, place):
        return remote(e3.at[k], place.at[me, x], gather_s.at[k], gather_r.at[k, x], plane3)

    @pl.when(x != 3)
    def _():
        to_plane3(0, E1).start()
        to_plane3(1, E2).start()

    for copy in own:
        copy.wait()

    def relay(bufs, recv):
        sent = [0, 0]
        pending = []
        y_at = (y, up(y, -1, 4), up(y, 1, 4), up(y, 2, 4))

        def go(t, dz, i, *tos):
            slot = up(z, dz, 8) * 4 + y_at[i]
            for to in tos:
                copy = remote(
                    bufs[t].at[slot], bufs[t].at[slot], send.at[t, sent[t]], recv.at[t, slot], to
                )
                copy.start()
                pending.append(copy)
                sent[t] += 1

        def came(t, dz, i):
            slot = up(z, dz, 8) * 4 + y_at[i]
            remote(
                bufs[t].at[slot], bufs[t].at[slot], send.at[t, 0], recv.at[t, slot], y_up
            ).wait_recv()

        def across(place):
            dz = (0, -1, 1, -2, 2, -3, 3, 4)[place]
            came(1, dz, 1)
            if place % 2 == 0:
                go(1, dz, 1, y_up)
            came(1, dz, 2)
            if place % 2 == 1:
                go(1, dz, 2, y_down)

        go(0, 0, 0, z_up, z_down, y_up, y_down)
        go(1, 0, 0, y_up, y_down, z_up, z_down)
        came(0, 0, 1)
        go(0, 0, 1, y_up, z_up, z_down)
        came(0, 0, 2)
        go(0, 0, 2, z_up, z_down)
        for r in (1, 2, 3):
            came(1, -r, 0)
            go(1, -r, 0, *((z_up,) if r < 3 else ()), y_up, y_down)
            came(1, r, 0)
            go(1, r, 0, z_down, y_up, y_down)
            if r == 1:
                across(0)
                came(0, 0, 3)
                go(0, 0, 3, z_up, z_down)
            for i in range(4):
                came(0, -r, i)
                if r < 3 or i % 2 == 0:
                    go(0, -r, i, z_up)
                came(0, r, i)
                if r < 3 or i % 2 == 1:
                    go(0, r, i, z_down)
                if r > 1 and i == 1:
                    across(2 * r - 3)
            if r > 1:
                across(2 * r - 2)
        came(1, 4, 0)
        go(1, 4, 0, y_up, y_down)
        for place in (5, 6, 7):
            across(place)
        for i in range(4):
            came(0, 4, i)
        for dz in (0, -1, 1, -2, 2, -3, 3, 4):
            came(1, dz, 3)
        for copy in pending:
            copy.wait_send()

    def exchange(mine, theirs, ssem, rsem, slot):
        copy = remote(mine.at[slot], theirs.at[slot], ssem.at[slot], rsem.at[slot], other)
        copy.start()
        copy.wait()
        return mine[slot] + theirs[slot]

    @pl.when(x == 3)
    def _():
        mine = [
            pltpu.make_async_copy(e3.at[0], E1.at[me, 3], own_sem.at[2]),
            pltpu.make_async_copy(e3.at[1], E2.at[me, 3], own_sem.at[3]),
            pltpu.make_async_copy(e3.at[2], E1.at[me, 4], own_sem.at[4]),
            pltpu.make_async_copy(
                img.at[c], henc.at[pl.ds(pl.multiple_of(c * 48, 16), 48)], own_sem.at[5]
            ),
        ]
        for copy in mine:
            copy.start()
        rows = remote(
            img.at[o], henc.at[pl.ds(pl.multiple_of(c * 48, 16), 48)], misc_s.at[0], misc_r.at[0], other
        )
        rows.start()
        for copy in mine:
            copy.wait()
        for from_x in range(3):
            for k, place in ((0, E1), (1, E2)):
                remote(
                    e3.at[k], place.at[me, from_x], gather_s.at[k], gather_r.at[k, from_x], x_next
                ).wait_recv()
        relay((E1, E2), recv_enc)
        rows.wait()

        def projected(slot, first, k):
            h = henc[...]
            weight = E1[pl.ds(first, BLOCKS), k].reshape(BLOCKS * 128, 128)
            es[slot, :, 0:128] = matmul(h, weight)
            squares = jnp.zeros((96, 128), F32)
            for j in range(BLOCKS):
                part = h[:, j * 128 : (j + 1) * 128].astype(F32)
                squares += part * part
            es[slot, :, 128:256] = squares
            total = exchange(es, er, xe_s, xe_r, slot)
            scale = lax.rsqrt(
                jnp.sum(total[:, 128:256], axis=-1, keepdims=True) * (1.0 / 3200) + EPSILON
            )
            return gelu(total[:, 0:128] * scale).astype(BF16)

        def layer(l, _):
            first, k = lax.rem(l, 2) * BLOCKS, l // 2
            activated = projected(lax.rem(l, 2), first, k)
            for j in range(0, BLOCKS, 2):
                weight = E2[pl.ds(first + j, 2), k].reshape(256, 128)
                branch = lax.dot_general(
                    activated, weight, (((1,), (1,)), ((), ())), preferred_element_type=F32
                )
                cols = slice(j * 128, (j + 2) * 128)
                henc[:, cols] = (henc[:, cols].astype(F32) + branch).astype(BF16)
            return 0

        lax.fori_loop(0, 8, layer, 0)
        lat[...] = projected(0, 0, 4)
        copy = remote(lat, latr, misc_s.at[1], misc_r.at[1], plane0)
        copy.start()
        copy.wait_send()

    def text_local(j):
        return pltpu.make_async_copy(
            text.at[:, pl.ds(pl.multiple_of(j * 512 + c * 256, 256), 256)],
            h0.at[c, :, pl.ds(j * 256, 256)],
            text_l.at[j],
        )

    def text_other(j):
        return remote(
            text.at[:, pl.ds(pl.multiple_of(j * 512 + o * 256, 256), 256)],
            h0.at[c, :, pl.ds(j * 256, 256)],
            text_s.at[j], text_r.at[j], other,
        )

    def text_came(j):
        return remote(
            text.at[:, pl.ds(0, 256)],
            h0.at[o, :, pl.ds(j * 256, 256)],
            text_s.at[j], text_r.at[j], other,
        )

    oh_local = pltpu.make_async_copy(oh, ohb.at[c], own_sem.at[2])
    oh_other = remote(oh, ohb.at[c], misc_s.at[0], misc_r.at[0], other)

    @pl.when(x == 0)
    def _():
        oh_local.start()
        oh_other.start()
        for j in range(BLOCKS):
            text_local(j).start()
            text_other(j).start()

    relay((A, B), recv_llm)

    @pl.when(x == 0)
    def _():
        oh_local.wait()
        oh_other.wait_send()
        remote(oh, ohb.at[o], misc_s.at[0], misc_r.at[0], other).wait_recv()
        for j in range(BLOCKS):
            text_local(j).wait()
            text_other(j).wait_send()
            text_came(j).wait_recv()
        remote(lat, latr, misc_s.at[1], misc_r.at[1], x_next).wait_recv()
        imgrows[96:128, :] = jnp.zeros((32, BLOCKS * 256), BF16)
        latent = latr[:, 0:64]
        for j in range(BLOCKS):
            imgrows[0:96, j * 256 : (j + 1) * 256] = matmul(latent, B[j, 512:576, :]).astype(BF16)

    def cols(j):
        return pl.ds(pl.multiple_of(j * 256, 256), 256)

    def folded(v):
        return v[:, 0:128] * v[:, 0:128] + v[:, 128:256] * v[:, 128:256]

    def activation(slot, acc, squares):
        xs[slot, :, 0:512] = acc
        xs[slot, :, 512:640] = squares
        total = exchange(xs, xr, x_s, x_r, slot)
        scale = lax.rsqrt(
            jnp.sum(total[:, 512:640], axis=-1, keepdims=True) * (1.0 / 8192) + EPSILON
        )
        return silu(total[:, 0:512] * scale).astype(BF16)

    zeros = (jnp.zeros((64, 512), F32), jnp.zeros((64, 128), F32))

    def flow(k):
        return remote(hin.at[k], hin.at[k], flow_s.at[k], flow_r.at[k], x_next)

    def result(k):
        return remote(osend.at[k], orecv.at[k], out_s.at[k], out_r.at[k], other)

    def emit(k):
        rows = pl.ds(pl.multiple_of(k * 32, 32), 32)
        for j in range(BLOCKS):
            span = slice(j * 256, (j + 1) * 256)
            out[rows, pl.ds(pl.multiple_of(j * 512 + c * 256, 256), 256)] = hin[
                k, pl.ds(pl.multiple_of(c * 32, 32), 32), span
            ]
        osend[k] = hin[k, pl.ds(pl.multiple_of(o * 32, 32), 32), :]
        result(k).start()

    def merge(k):
        result(k).wait_recv()
        rows = pl.ds(pl.multiple_of(k * 32, 32), 32)
        for j in range(BLOCKS):
            out[rows, pl.ds(pl.multiple_of(j * 512 + o * 256, 256), 256)] = orecv[
                k, :, j * 256 : (j + 1) * 256
            ]

    def chunk(k, _):
        rows = pl.ds(pl.multiple_of(k * 32, 32), 32)

        @pl.when(x == 0)
        def _():
            marks = jnp.concatenate([ohb[0, rows, :], ohb[1, rows, :]], axis=0)
            hit = jnp.sum(marks.astype(F32), axis=-1, keepdims=True) > 0.5
            for j in range(BLOCKS):
                span = slice(j * 256, (j + 1) * 256)
                placed = matmul(marks, imgrows[:, span])
                words = jnp.concatenate([h0[0, rows, span], h0[1, rows, span]], axis=0)
                hin[k, :, span] = jnp.where(hit, placed, words.astype(F32)).astype(BF16)

        @pl.when(x > 0)
        def _():
            flow(k).wait_recv()

        def first(j, carry):
            acc, squares = carry
            h = hin[k, :, cols(j)]
            return acc + matmul(h, A[j]), squares + folded(h.astype(F32))

        a = activation(0, *lax.fori_loop(0, BLOCKS, first, zeros, unroll=4))

        def second(j, carry):
            acc, squares = carry
            h = hin[k, :, cols(j)].astype(F32) + matmul(a, B[j, 0:512, :])
            h = h.astype(BF16)
            hin[k, :, cols(j)] = h
            return acc + matmul(h, A[BLOCKS + j]), squares + folded(h.astype(F32))

        carry = lax.fori_loop(0, BLOCKS, second, zeros, unroll=4)

        @pl.when(z_hi == 0)
        def _():
            emit(k)

        b = activation(1, *carry)

        def third(j, _):
            h = hin[k, :, cols(j)].astype(F32) + matmul(b, B[BLOCKS + j, 0:512, :])
            hin[k, :, cols(j)] = h.astype(BF16)
            return 0

        lax.fori_loop(0, BLOCKS, third, 0, unroll=4)

        @pl.when(x < 3)
        def _():
            flow(k).start()

        @pl.when(z_hi == 1)
        def _():
            emit(k)

        @pl.when(k > 0)
        def _():
            merge(k - 1)

        return 0

    lax.fori_loop(0, CHUNKS, chunk, 0)
    merge(CHUNKS - 1)

    def drain(k, _):
        result(k).wait_send()

        @pl.when(x < 3)
        def _():
            flow(k).wait_send()

        return 0

    lax.fori_loop(0, CHUNKS, drain, 0)

    @pl.when(x != 3)
    def _():
        to_plane3(0, E1).wait_send()
        to_plane3(1, E2).wait_send()


def local(text, image, positions, enc_in, enc_out, conn_in, conn_out, llm_in, llm_out):
    core = lax.rem(lax.axis_index("dp"), 2)
    wb = jnp.concatenate([llm_out[0], conn_out], axis=0)
    e3 = jnp.stack(
        [
            jnp.pad(enc_in[0], ((0, 28), (0, 0))),
            jnp.pad(enc_out[0].T, ((0, 28), (0, 0))),
            jnp.pad(conn_in, ((0, 28), (0, 64))),
        ]
    )
    img = jnp.pad(image.reshape(48, 16, 2, 100), ((0, 0), (0, 0), (0, 0), (0, 28)))
    img = img.transpose(2, 0, 1, 3).reshape(2, 48, 2048)
    row = lax.broadcasted_iota(jnp.int32, (192, 48), 0)
    spots = (positions + 64 * jnp.arange(3, dtype=jnp.int32)[:, None]).reshape(1, 48)
    marks = (spots == row).astype(BF16)
    blank = jnp.zeros((192, 48), BF16)
    oh = jnp.concatenate(
        [
            jnp.where(core == 0, marks, blank),
            jnp.where(core == 1, marks, blank),
            jnp.zeros((192, 32), BF16),
        ],
        axis=1,
    )
    any_spec = pl.BlockSpec(memory_space=pl.ANY)
    dma = pltpu.SemaphoreType.DMA
    hidden = pl.pallas_call(
        kernel,
        out_shape=jax.ShapeDtypeStruct((192, 8192), BF16),
        in_specs=[any_spec] * 6,
        out_specs=pl.BlockSpec(memory_space=pltpu.VMEM),
        scratch_shapes=[
            pltpu.VMEM((32, 256, 512), BF16),
            pltpu.VMEM((32, 576, 256), BF16),
            pltpu.VMEM((32, 5, 128, 128), BF16),
            pltpu.VMEM((32, 4, 128, 128), BF16),
            pltpu.VMEM((2, 192, 4096), BF16),
            pltpu.VMEM((2, 192, 128), BF16),
            pltpu.VMEM((96, 2048), BF16),
            pltpu.VMEM((96, 128), BF16),
            pltpu.VMEM((96, 128), BF16),
            pltpu.VMEM((128, 4096), BF16),
            pltpu.VMEM((2, 64, 640), F32),
            pltpu.VMEM((2, 64, 640), F32),
            pltpu.VMEM((2, 96, 256), F32),
            pltpu.VMEM((2, 96, 256), F32),
            pltpu.VMEM((CHUNKS, 64, 4096), BF16),
            pltpu.VMEM((CHUNKS, 32, 4096), BF16),
            pltpu.VMEM((CHUNKS, 32, 4096), BF16),
            dma((2, 31)),
            dma((2, 32)),
            dma((2, 32)),
            dma((6,)),
            dma((2,)),
            dma((2, 4)),
            dma((16,)),
            dma((16,)),
            dma((16,)),
            dma((2,)),
            dma((2,)),
            dma((2,)),
            dma((2,)),
            dma((2,)),
            dma((2,)),
            dma((CHUNKS,)),
            dma((CHUNKS,)),
            dma((CHUNKS,)),
            dma((CHUNKS,)),
        ],
        compiler_params=pltpu.CompilerParams(
            collective_id=0, has_side_effects=True, vmem_limit_bytes=60 * 1024 * 1024
        ),
        cost_estimate=pl.CostEstimate(
            flops=14_000_000_000, bytes_accessed=16_000_000, transcendentals=1_000_000
        ),
    )(text, llm_in[0], wb, e3, img, oh)
    return hidden[None]


def solution(mesh):
    return jax.shard_map(
        local,
        mesh=mesh,
        in_specs=(
            P("dp", None),
            P("dp", None),
            P("dp", None),
            P("section", "dp", None),
            P("section", None, "dp"),
            P("dp", None),
            P(None, "dp"),
            P("section", "dp", None),
            P("section", None, "dp"),
        ),
        out_specs=P("section", "dp", None),
        check_vma=False,
    )
```

time: 784 us -> 273 us (0.35)
  the two profiles are of different devices: /device:TPU:44 before, /device:TPU:7 now
where the time goes in v1:
time: 273 us; the launch traced here: 271 us
  Pallas kernels  258 us (95%)
  local copies, waits for them, and re-layouts  9.81 us (4%)
  other arithmetic  3.84 us (1%)
    pallas_call x1, Pallas kernels, local(): pl.pallas_call(kernel, out_shape=jax.ShapeDtypeStruct((192, 8192), BF16),...  258 us

profile of v1, /device:TPU:7, one launch (start us, length us, event | category | flops | bytes accessed | tf_op | source)
XLA Modules:
  0.0 271.3 jit_solution(14737414584943864229)
XLA Ops:
  0.0 0.1 pad.21.clone
  0.1 0.8 broadcast_add_fusion
  0.8 0.1 eq.17
  0.9 0.8 copy.10
  1.7 0.8 pad_bitcast_fusion.3
  2.5 0.8 pad_bitcast_fusion.1
  3.3 0.6 pad_maximum_fusion.1.e3
  3.9 0.7 maximum_maximum_fusion.oh
  4.6 1.7 pad_maximum_fusion.wb
  6.4 2.4 reshape.13
  8.8 0.1 copy.11
  8.8 0.1 pad_bitcast_fusion
  8.9 0.9 reshape.14.img
  9.8 257.6 %shard_map.91 = bf16[192,8192]{1,0:T(8,128)(2,1)} custom-call(bf16[192,8192]{1,0:T(8,128)(2,1)} %text.1, bf16[256,512]{1,0:T(8,128)(2,1)} %bitcast.21, bf16[576,256]{1,0:T(8,128)(2,1)} %pad_maximum_fusion.wb, bf16[3,128,128]{2,1,0:T(8,128)(2,1)} %pad_maximum_fusion.1.e3, bf16[2,48,2048]{2,1,0:T(8,128)(2,1)} %reshape.14.img, ...), custom_call_target="tpu_custom_call" | custom-call | flops 14000000000 | bytes 16000000 | tf_op jit(solution)/shard_map/pallas_call | solution.py:415
  267.4 3.9 %copy.13 = bf16[1,192,8192]{2,1,0:T(8,128)(2,1)} copy(bf16[1,192,8192]{2,1,0:T(8,128)(2,1)} %bitcast.17) | data formatting | bytes 6291456
  (3 shorter events, 0.0 us)

commit v2 on v1

v2 whole, which is shorter than its diff:
```python
import jax
import jax.numpy as jnp
from jax import lax
from jax.experimental import pallas as pl
from jax.experimental.pallas import tpu as pltpu
from jax.sharding import PartitionSpec as P

EPSILON = 1e-06
MESH = pl.DeviceIdType.MESH
F32 = jnp.float32
BF16 = jnp.bfloat16
SPLIT = 208
TURNS = ((1, 0.15), (2, 0.35), (3, 0.55))
BLOCKS = 16


def gelu(v):
    return 0.5 * v * (1.0 + lax.erf(v * 0.7071067811865476))


def silu(v):
    return v / (1.0 + jnp.exp(-v))


def matmul(a, b):
    return jnp.dot(a, b, preferred_element_type=F32)


def device(x, y, z, c):
    return (x * 2 + z // 4, lax.rem(z, 4) * 8 + y * 2 + c)


def kernel(
    text, image, positions, enc_in, enc_out, conn_in, conn_out, wa, wb, out,
    A, B, E1, E2, C1, C2, h0, ohb, img2, henc, imgrows, xs, xr, es, er, hin, osend, orecv,
    send_llm, recv_llm, send_enc, recv_enc, recv_conn, own_sem, text_l, text_s, text_r,
    misc_s, misc_r, x_s, x_r, xe_s, xe_r, flow_s, flow_r, out_s, out_r,
):
    section = lax.axis_index("section")
    dp = lax.axis_index("dp")
    x, z_hi = section // 2, lax.rem(section, 2)
    z = z_hi * 4 + dp // 8
    y = lax.rem(dp // 2, 4)
    c = lax.rem(dp, 2)
    o = 1 - c
    me = z * 4 + y

    def up(v, by, n):
        return lax.rem(v + by + n, n)

    y_up, y_down = device(x, up(y, 1, 4), z, c), device(x, up(y, -1, 4), z, c)
    z_up, z_down = device(x, y, up(z, 1, 8), c), device(x, y, up(z, -1, 8), c)
    other = device(x, y, z, o)
    x_next = device(up(x, 1, 4), y, z, c)
    x_last = device(up(x, -1, 4), y, z, c)

    def remote(src, dst, ssem, rsem, to):
        return pltpu.make_async_remote_copy(
            src_ref=src, dst_ref=dst, send_sem=ssem, recv_sem=rsem, device_id=to, device_id_type=MESH
        )

    barrier = pltpu.get_barrier_semaphore()
    for to in (y_up, y_down, z_up, z_down, other, x_next, x_last):
        pl.semaphore_signal(barrier, inc=1, device_id=to, device_id_type=MESH)

    own = [
        pltpu.make_async_copy(wa, A.at[me], own_sem.at[0]),
        pltpu.make_async_copy(wb, B.at[me], own_sem.at[1]),
    ]
    for copy in own:
        copy.start()
    blank = jnp.zeros((128, 128), BF16)
    E1[me] = blank
    E2[me] = blank
    E1[me, 0:100, :] = enc_in[...]
    E2[me, :, 0:100] = enc_out[...]

    @pl.when(x == 3)
    def _():
        C1[me] = blank
        C1[me, 0:100, 0:64] = conn_in[...]
        C2[me] = conn_out[...]

    pl.semaphore_wait(barrier, 7)

    def relay(groups, send, recv):
        first_of = (0, len(groups[0]))
        sent = [0, 0]
        pending = []
        steps = []
        y_at = (y, up(y, -1, 4), up(y, 1, 4), up(y, 2, 4))

        def copies(t, dz, i, number, to):
            slot = up(z, dz, 8) * 4 + y_at[i]
            return [
                remote(
                    part(slot), part(slot),
                    send.at[first_of[t] + e, number], recv.at[first_of[t] + e, slot], to,
                )
                for e, part in enumerate(groups[t])
            ]

        def go(t, dz, i, *tos):
            for to in tos:
                for copy in copies(t, dz, i, sent[t], to):
                    copy.start()
                    pending.append(copy)
                sent[t] += 1

        def came(t, dz, i, *tos):
            def step():
                for copy in copies(t, dz, i, 0, y_up):
                    copy.wait_recv()
                go(t, dz, i, *tos)

            steps.append(step)

        def across(place):
            dz = (0, -1, 1, -2, 2, -3, 3, 4)[place]
            came(1, dz, 1, *((y_up,) if place % 2 == 0 else ()))
            came(1, dz, 2, *((y_down,) if place % 2 == 1 else ()))

        def start():
            go(0, 0, 0, z_up, z_down, y_up, y_down)
            go(1, 0, 0, y_up, y_down, z_up, z_down)

        came(0, 0, 1, y_up, z_up, z_down)
        came(0, 0, 2, z_up, z_down)
        for r in (1, 2, 3):
            came(1, -r, 0, *((z_up,) if r < 3 else ()), y_up, y_down)
            came(1, r, 0, z_down, y_up, y_down)
            if r == 1:
                across(0)
                came(0, 0, 3, z_up, z_down)
            for i in range(4):
                came(0, -r, i, *((z_up,) if r < 3 or i % 2 == 0 else ()))
                came(0, r, i, *((z_down,) if r < 3 or i % 2 == 1 else ()))
                if r > 1 and i == 1:
                    across(2 * r - 3)
            if r > 1:
                across(2 * r - 2)
        came(1, 4, 0, y_up, y_down)
        for place in (5, 6, 7):
            across(place)
        for i in range(4):
            came(0, 4, i)
        for dz in (0, -1, 1, -2, 2, -3, 3, 4):
            came(1, dz, 3)

        def finish():
            for copy in pending:
                copy.wait_send()

        return start, steps, finish

    def exchange(mine, theirs, ssem, rsem, slot):
        copy = remote(mine, theirs, ssem.at[slot], rsem.at[slot], other)
        copy.start()
        copy.wait()
        return mine[...] + theirs[...]

    enc_start, enc_steps, enc_finish = relay(
        ((lambda s: E1.at[s],), (lambda s: E2.at[s],)), send_enc, recv_enc
    )
    llm_start, llm_steps, llm_finish = relay(
        (
            (lambda s: A.at[s, pl.ds(0, SPLIT)],),
            (lambda s: B.at[s], lambda s: A.at[s, pl.ds(SPLIT, 256 - SPLIT)]),
        ),
        send_llm, recv_llm,
    )
    enc_start()
    for copy in own:
        copy.wait()
    llm_start()

    def text_local(j):
        return pltpu.make_async_copy(
            text.at[:, pl.ds(pl.multiple_of(j * 512 + c * 256, 256), 256)],
            h0.at[c, :, pl.ds(j * 256, 256)],
            text_l.at[j],
        )

    def text_other(j):
        return remote(
            text.at[:, pl.ds(pl.multiple_of(j * 512 + o * 256, 256), 256)],
            h0.at[c, :, pl.ds(j * 256, 256)],
            text_s.at[j], text_r.at[j], other,
        )

    def text_came(j):
        return remote(
            text.at[:, pl.ds(0, 256)],
            h0.at[o, :, pl.ds(j * 256, 256)],
            text_s.at[j], text_r.at[j], other,
        )

    own_rows = pl.ds(pl.multiple_of(c * 48, 16), 48)
    other_rows = pl.ds(pl.multiple_of(o * 48, 16), 48)
    image_other = remote(img2.at[o], henc.at[own_rows], misc_s.at[0], misc_r.at[0], other)
    marks_other = remote(ohb.at[c], ohb.at[c], misc_s.at[1], misc_r.at[1], other)

    @pl.when(x == 0)
    def _():
        spread = lax.broadcasted_iota(jnp.int32, (256, 128), 0)
        lane = lax.broadcasted_iota(jnp.int32, (256, 128), 1)
        for b in range(2 * BLOCKS):
            base = 100 * b // 128 * 128
            width = min(256, 3200 - base)
            pick = (spread == lane + (100 * b - base)) & (lane < 100)
            pick = jnp.where(pick, 1.0, 0.0).astype(BF16)[0:width]
            block = matmul(image[:, base : base + width], pick).astype(BF16)
            img2[b % 2, :, b // 2 * 128 : (b // 2 + 1) * 128] = block
        image_other.start()
        henc[own_rows, :] = img2[c]
        spot = jnp.full((1, 128), -1.0, F32)
        for m in range(3):
            j = lax.broadcasted_iota(jnp.int32, (16, 128), 0)
            at = lax.broadcasted_iota(jnp.int32, (16, 128), 1)
            pick = jnp.where(at == j + (m * 16 + c * 48), 1.0, 0.0).astype(BF16)
            rows = (positions[m : m + 1, :] + (64 * m + 1)).astype(F32).astype(BF16)
            spot += matmul(jnp.broadcast_to(rows, (16, 16)), pick)[0:1]
        row = lax.broadcasted_iota(jnp.int32, (192, 128), 0).astype(F32)
        ohb[c] = jnp.where(row == spot, 1.0, 0.0).astype(BF16)
        marks_other.start()
        for j in range(BLOCKS):
            text_local(j).start()
            text_other(j).start()

    for step in enc_steps:
        step()
    enc_finish()

    conn_start, conn_steps, conn_finish = relay(
        ((lambda s: C1.at[s],), (lambda s: C2.at[s],)), send_enc, recv_conn
    )

    @pl.when(x == 3)
    def _():
        conn_start()
        for step in conn_steps:
            step()
        conn_finish()

    def projected(slot, weight):
        h = henc[...]
        es[slot, :, 0:128] = matmul(h, weight.reshape(BLOCKS * 128, 128))
        squares = jnp.zeros((96, 128), F32)
        for j in range(BLOCKS):
            part = h[:, j * 128 : (j + 1) * 128].astype(F32)
            squares += part * part
        es[slot, :, 128:256] = squares
        total = exchange(es.at[slot], er.at[slot], xe_s, xe_r, slot)
        scale = lax.rsqrt(
            jnp.sum(total[:, 128:256], axis=-1, keepdims=True) * (1.0 / 3200) + EPSILON
        )
        return gelu(total[:, 0:128] * scale).astype(BF16)

    passed = remote(henc, henc, misc_s.at[2], misc_r.at[2], x_next)
    pictures = remote(
        imgrows.at[pl.ds(0, 96)], imgrows.at[pl.ds(0, 96)], misc_s.at[3], misc_r.at[3], x_next
    )

    def encoder(plane):
        @pl.when(x == plane)
        def _():
            if plane == 0:
                image_other.wait_send()
                remote(
                    img2.at[c], henc.at[other_rows], misc_s.at[0], misc_r.at[0], other
                ).wait_recv()
            else:
                passed.wait_recv()

            def layer(l, _):
                activated = projected(l, E1[pl.ds(l * BLOCKS, BLOCKS)])
                for j in range(BLOCKS):
                    branch = matmul(activated, E2[l * BLOCKS + j])
                    span = slice(j * 128, (j + 1) * 128)
                    henc[:, span] = (henc[:, span].astype(F32) + branch).astype(BF16)
                return 0

            lax.fori_loop(0, 2, layer, 0)
            if plane < 3:
                passed.start()
            else:
                latent = projected(0, C1[0:BLOCKS])[:, 0:64]
                for j in range(BLOCKS):
                    imgrows[0:96, j * 256 : (j + 1) * 256] = matmul(latent, C2[j]).astype(BF16)
                pictures.start()

    encoder(0)
    turns = {int(len(llm_steps) * part): plane for plane, part in TURNS}
    for number, step in enumerate(llm_steps):
        if number in turns:
            encoder(turns[number])
        step()
    llm_finish()

    @pl.when(x == 0)
    def _():
        marks_other.wait_send()
        remote(ohb.at[o], ohb.at[o], misc_s.at[1], misc_r.at[1], other).wait_recv()
        for j in range(BLOCKS):
            text_local(j).wait()
            text_other(j).wait_send()
            text_came(j).wait_recv()
        imgrows[96:128, :] = jnp.zeros((32, BLOCKS * 256), BF16)
        pictures.wait_recv()

    @pl.when(x == 3)
    def _():
        pictures.wait_send()

    @pl.when(x < 3)
    def _():
        passed.wait_send()

    def cols(j):
        return slice(j * 256, (j + 1) * 256)

    def folded(v):
        return v[:, 0:128] * v[:, 0:128] + v[:, 128:256] * v[:, 128:256]

    def activation(slot, size, acc, squares):
        mine = xs.at[slot, pl.ds(0, size)]
        mine[:, 0:512] = acc
        mine[:, 512:640] = squares
        total = exchange(mine, xr.at[slot, pl.ds(0, size)], x_s, x_r, slot)
        scale = lax.rsqrt(
            jnp.sum(total[:, 512:640], axis=-1, keepdims=True) * (1.0 / 8192) + EPSILON
        )
        return silu(total[:, 0:512] * scale).astype(BF16)

    def chunk(k, start, count, merge_last):
        size = 2 * count
        base = pl.multiple_of(2 * start, size)
        rows = pl.ds(pl.multiple_of(start, count), count)
        both = pl.ds(base, size)
        mine = pl.ds(pl.multiple_of(base + c * count, count), count)
        theirs = pl.ds(pl.multiple_of(base + o * count, count), count)

        def flow(part):
            span = hin.at[both, pl.ds(part * 1024, 1024)]
            return remote(span, span, flow_s.at[k, part], flow_r.at[k, part], x_next)

        def emit():
            for j in range(BLOCKS):
                out[rows, pl.ds(pl.multiple_of(j * 512 + c * 256, 256), 256)] = hin[mine, cols(j)]
            osend[rows, :] = hin[theirs, :]
            result(k, start, count).start()

        @pl.when(x == 0)
        def _():
            marks = jnp.concatenate([ohb[0, rows, :], ohb[1, rows, :]], axis=0)
            hit = jnp.sum(marks.astype(F32), axis=-1, keepdims=True) > 0.5
            for j in range(BLOCKS):
                placed = matmul(marks, imgrows[:, cols(j)])
                words = jnp.concatenate([h0[0, rows, cols(j)], h0[1, rows, cols(j)]], axis=0)
                hin[both, cols(j)] = jnp.where(hit, placed, words.astype(F32)).astype(BF16)

        acc, squares = jnp.zeros((size, 512), F32), jnp.zeros((size, 128), F32)
        for part in range(4):

            @pl.when(x > 0)
            def _():
                flow(part).wait_recv()

            for j in range(4 * part, 4 * part + 4):
                h = hin[both, cols(j)]
                acc, squares = acc + matmul(h, A[j]), squares + folded(h.astype(F32))
        a = activation(0, size, acc, squares)
        acc, squares = jnp.zeros((size, 512), F32), jnp.zeros((size, 128), F32)
        for j in range(BLOCKS):
            h = (hin[both, cols(j)].astype(F32) + matmul(a, B[j])).astype(BF16)
            hin[both, cols(j)] = h
            acc, squares = acc + matmul(h, A[BLOCKS + j]), squares + folded(h.astype(F32))

        @pl.when(z_hi == 0)
        def _():
            emit()

        b = activation(1, size, acc, squares)
        for part in range(4):
            for j in range(4 * part, 4 * part + 4):
                h = hin[both, cols(j)].astype(F32) + matmul(b, B[BLOCKS + j])
                hin[both, cols(j)] = h.astype(BF16)

            @pl.when(x < 3)
            def _():
                flow(part).start()

        @pl.when(z_hi == 1)
        def _():
            emit()

        merge_last()

        def drain():
            result(k, start, count).wait_send()

            @pl.when(x < 3)
            def _():
                for part in range(4):
                    flow(part).wait_send()

        return drain

    def result(k, start, count):
        rows = pl.ds(pl.multiple_of(start, count), count)
        return remote(osend.at[rows], orecv.at[rows], out_s.at[k], out_r.at[k], other)

    def merge(k, start, count):
        result(k, start, count).wait_recv()
        rows = pl.ds(pl.multiple_of(start, count), count)
        for j in range(BLOCKS):
            out[rows, pl.ds(pl.multiple_of(j * 512 + o * 256, 256), 256)] = orecv[rows, cols(j)]

    def full(k, _):
        def merge_last():
            @pl.when(k > 0)
            def _():
                merge(k - 1, (k - 1) * 32, 32)

        chunk(k, k * 32, 32, merge_last)
        return 0

    lax.fori_loop(0, 5, full, 0)
    half = [
        chunk(5, 160, 16, lambda: merge(4, 128, 32)),
        chunk(6, 176, 16, lambda: merge(5, 160, 16)),
    ]
    merge(6, 176, 16)

    def drain(k, _):
        result(k, k * 32, 32).wait_send()

        @pl.when(x < 3)
        def _():
            for part in range(4):
                span = hin.at[
                    pl.ds(pl.multiple_of(k * 64, 64), 64), pl.ds(part * 1024, 1024)
                ]
                remote(span, span, flow_s.at[k, part], flow_r.at[k, part], x_next).wait_send()

        return 0

    lax.fori_loop(0, 5, drain, 0)
    for finish in half:
        finish()


def local(text, image, positions, enc_in, enc_out, conn_in, conn_out, llm_in, llm_out):
    any_spec = pl.BlockSpec(memory_space=pl.ANY)
    vmem_spec = pl.BlockSpec(memory_space=pltpu.VMEM)
    dma = pltpu.SemaphoreType.DMA
    hidden = pl.pallas_call(
        kernel,
        out_shape=jax.ShapeDtypeStruct((192, 8192), BF16),
        in_specs=[any_spec] + [vmem_spec] * 6 + [any_spec] * 2,
        out_specs=vmem_spec,
        scratch_shapes=[
            pltpu.VMEM((32, 256, 512), BF16),
            pltpu.VMEM((32, 512, 256), BF16),
            pltpu.VMEM((32, 128, 128), BF16),
            pltpu.VMEM((32, 128, 128), BF16),
            pltpu.VMEM((32, 128, 128), BF16),
            pltpu.VMEM((32, 64, 256), BF16),
            pltpu.VMEM((2, 192, 4096), BF16),
            pltpu.VMEM((2, 192, 128), BF16),
            pltpu.VMEM((2, 48, 2048), BF16),
            pltpu.VMEM((96, 2048), BF16),
            pltpu.VMEM((128, 4096), BF16),
            pltpu.VMEM((2, 64, 640), F32),
            pltpu.VMEM((2, 64, 640), F32),
            pltpu.VMEM((2, 96, 256), F32),
            pltpu.VMEM((2, 96, 256), F32),
            pltpu.VMEM((384, 4096), BF16),
            pltpu.VMEM((192, 4096), BF16),
            pltpu.VMEM((192, 4096), BF16),
            dma((3, 31)),
            dma((3, 32)),
            dma((2, 31)),
            dma((2, 32)),
            dma((2, 32)),
            dma((2,)),
            dma((16,)),
            dma((16,)),
            dma((16,)),
            dma((4,)),
            dma((4,)),
            dma((2,)),
            dma((2,)),
            dma((2,)),
            dma((2,)),
            dma((7, 4)),
            dma((7, 4)),
            dma((7,)),
            dma((7,)),
        ],
        compiler_params=pltpu.CompilerParams(
            collective_id=0, has_side_effects=True, vmem_limit_bytes=60 * 1024 * 1024
        ),
        cost_estimate=pl.CostEstimate(
            flops=14_000_000_000, bytes_accessed=16_000_000, transcendentals=1_000_000
        ),
    )(text, image, positions, enc_in[0], enc_out[0], conn_in, conn_out, llm_in[0], llm_out[0])
    return hidden[None]


def solution(mesh):
    return jax.shard_map(
        local,
        mesh=mesh,
        in_specs=(
            P("dp", None),
            P("dp", None),
            P("dp", None),
            P("section", "dp", None),
            P("section", None, "dp"),
            P("dp", None),
            P(None, "dp"),
            P("section", "dp", None),
            P("section", None, "dp"),
        ),
        out_specs=P("section", "dp", None),
        check_vma=False,
    )
```

time: 273 us -> 289 us (1.059)
  Pallas kernels: 258 us -> 282 us
  other arithmetic: 3.84 us -> 0 us
  local copies, waits for them, and re-layouts: 9.81 us -> 6.74 us
    pallas_call x1, Pallas kernels: 258 us -> 282 us  [local(): pl.pallas_call(kernel, out_shape=jax.ShapeDtypeStruct((192, 8192), BF16),...]
    reshape x3 -> x0, local copies, waits for them, and re-layouts: 3.37 us -> none  [the longest x2 2.46 us: local(): image.reshape(48, 16, 2, 100)]
    unnamed x2 -> x3, local copies, waits for them, and re-layouts: 4.68 us -> 6.74 us
where the time goes in v2:
time: 289 us; the launch traced here: 288 us
  Pallas kernels  282 us (98%)
  local copies, waits for them, and re-layouts  6.74 us (2%)
    pallas_call x1, Pallas kernels, local(): pl.pallas_call(kernel, out_shape=jax.ShapeDtypeStruct((192, 8192), BF16),...  282 us
    unnamed x3, local copies, waits for them, and re-layouts  6.74 us

profile of v2, /device:TPU:7, one launch (start us, length us, event | category | flops | bytes accessed | tf_op | source)
XLA Modules:
  0.0 288.3 jit_solution(14520435862364364648)
XLA Ops:
  0.0 1.4 copy.11.conn_in
  1.4 1.5 copy.10
  2.9 281.5 %shard_map.91 = bf16[192,8192]{1,0:T(8,128)(2,1)} custom-call(bf16[192,8192]{1,0:T(8,128)(2,1)} %text.1, bf16[48,3200]{1,0:T(8,128)(2,1)} %image.1, s32[3,16]{1,0:T(4,128)} %positions.1, bf16[100,128]{1,0:T(8,128)(2,1)} %bitcast.9, bf16[128,100]{1,0:T(8,128)(2,1)} %bitcast.6, bf16[100,64]{1,0:T(8,128)(2,1)} %copy.11.conn_in, bf16[64,256]{1,0:T(8,128)(2,1)} %conn_out.1, ...), custom_call_target="tpu_custom_call" | custom-call | flops 14000000000 | bytes 16000000 | tf_op jit(solution)/shard_map/pallas_call | solution.py:457
  284.4 3.9 %copy.13 = bf16[1,192,8192]{2,1,0:T(8,128)(2,1)} copy(bf16[1,192,8192]{2,1,0:T(8,128)(2,1)} %bitcast.5) | data formatting | bytes 6291456

commit v3 on v2

--- a/solution.py
+++ b/solution.py
@@ -9,8 +9,8 @@
 MESH = pl.DeviceIdType.MESH
 F32 = jnp.float32
 BF16 = jnp.bfloat16
-SPLIT = 208
-TURNS = ((1, 0.15), (2, 0.35), (3, 0.55))
+SPLIT = 192
+TURN = 8
 BLOCKS = 16
 
 
@@ -32,8 +32,8 @@
 
 def kernel(
     text, image, positions, enc_in, enc_out, conn_in, conn_out, wa, wb, out,
-    A, B, E1, E2, C1, C2, h0, ohb, img2, henc, imgrows, xs, xr, es, er, hin, osend, orecv,
-    send_llm, recv_llm, send_enc, recv_enc, recv_conn, own_sem, text_l, text_s, text_r,
+    A, B, E1, E2, C1, C2, ep, h0, ohb, img2, henc, imgrows, xs, xr, es, er, hin, osend, orecv,
+    send_llm, recv_llm, send_enc, recv_enc, gather_s, gather_r, own_sem, text_l, text_s, text_r,
     misc_s, misc_r, x_s, x_r, xe_s, xe_r, flow_s, flow_r, out_s, out_r,
 ):
     section = lax.axis_index("section")
@@ -60,7 +60,7 @@
         )
 
     barrier = pltpu.get_barrier_semaphore()
-    for to in (y_up, y_down, z_up, z_down, other, x_next, x_last):
+    for to in (y_up, y_down, z_up, z_down, other, x_next, x_last, device(up(x, 2, 4), y, z, c)):
         pl.semaphore_signal(barrier, inc=1, device_id=to, device_id_type=MESH)
 
     own = [
@@ -70,18 +70,35 @@
     for copy in own:
         copy.start()
     blank = jnp.zeros((128, 128), BF16)
-    E1[me] = blank
-    E2[me] = blank
-    E1[me, 0:100, :] = enc_in[...]
-    E2[me, :, 0:100] = enc_out[...]
+    ep[0] = blank
+    ep[1] = blank
+    ep[0, 0:100, :] = enc_in[...]
+    ep[1, :, 0:100] = enc_out[...]
 
     @pl.when(x == 3)
     def _():
         C1[me] = blank
         C1[me, 0:100, 0:64] = conn_in[...]
         C2[me] = conn_out[...]
-
-    pl.semaphore_wait(barrier, 7)
+        E1[me, 1] = ep[0]
+        E2[me, 1] = ep[1]
+
+    pl.semaphore_wait(barrier, 8)
+
+    def gathered(source):
+        to = device(max(2, source + 1), y, z, c)
+        k = source % 2
+        return [
+            remote(ep.at[e], place.at[me, k], gather_s.at[e], gather_r.at[e, k], to)
+            for e, place in ((0, E1), (1, E2))
+        ]
+
+    for source in range(3):
+
+        @pl.when(x == source)
+        def _():
+            for copy in gathered(source):
+                copy.start()
 
     def relay(groups, send, recv):
         first_of = (0, len(groups[0]))
@@ -121,27 +138,52 @@
             came(1, dz, 2, *((y_down,) if place % 2 == 1 else ()))
 
         def start():
-            go(0, 0, 0, z_up, z_down, y_up, y_down)
-            go(1, 0, 0, y_up, y_down, z_up, z_down)
+            go(1, 0, 0, z_up, z_down)
+            go(0, 0, 0, y_up, y_down, z_up, z_down)
+            go(1, 0, 0, y_up, y_down)
 
         came(0, 0, 1, y_up, z_up, z_down)
         came(0, 0, 2, z_up, z_down)
-        for r in (1, 2, 3):
-            came(1, -r, 0, *((z_up,) if r < 3 else ()), y_up, y_down)
-            came(1, r, 0, z_down, y_up, y_down)
-            if r == 1:
-                across(0)
-                came(0, 0, 3, z_up, z_down)
-            for i in range(4):
-                came(0, -r, i, *((z_up,) if r < 3 or i % 2 == 0 else ()))
-                came(0, r, i, *((z_down,) if r < 3 or i % 2 == 1 else ()))
-                if r > 1 and i == 1:
-                    across(2 * r - 3)
-            if r > 1:
-                across(2 * r - 2)
+        came(1, -1, 0, z_up, y_up, y_down)
+        came(1, 1, 0, z_down, y_up, y_down)
+        came(0, 0, 3, z_up, z_down)
+        across(0)
+        came(0, -1, 0, z_up)
+        came(0, 1, 0, z_down)
+        came(1, -2, 0, z_up, y_up, y_down)
+        came(1, 2, 0, z_down, y_up, y_down)
+        came(0, -1, 1, z_up)
+        came(0, 1, 1, z_down)
+        across(1)
+        came(0, -1, 2, z_up)
+        came(0, 1, 2, z_down)
+        came(1, -3, 0, y_up, y_down)
+        came(1, 3, 0, z_down, y_up, y_down)
+        across(2)
+        came(0, -1, 3, z_up)
+        came(0, 1, 3, z_down)
+        came(0, -2, 0, z_up)
+        came(0, 2, 0, z_down)
+        across(3)
         came(1, 4, 0, y_up, y_down)
-        for place in (5, 6, 7):
-            across(place)
+        came(0, -2, 1, z_up)
+        came(0, 2, 1, z_down)
+        across(4)
+        came(0, -2, 2, z_up)
+        came(0, 2, 2, z_down)
+        across(5)
+        came(0, -2, 3, z_up)
+        came(0, 2, 3, z_down)
+        came(0, -3, 0, z_up)
+        came(0, 3, 0)
+        across(6)
+        came(0, -3, 1)
+        came(0, 3, 1, z_down)
+        came(0, -3, 2, z_up)
+        came(0, 3, 2)
+        across(7)
+        came(0, -3, 3)
+        came(0, 3, 3, z_down)
         for i in range(4):
             came(0, 4, i)
         for dz in (0, -1, 1, -2, 2, -3, 3, 4):
@@ -159,9 +201,6 @@
         copy.wait()
         return mine[...] + theirs[...]
 
-    enc_start, enc_steps, enc_finish = relay(
-        ((lambda s: E1.at[s],), (lambda s: E2.at[s],)), send_enc, recv_enc
-    )
     llm_start, llm_steps, llm_finish = relay(
         (
             (lambda s: A.at[s, pl.ds(0, SPLIT)],),
@@ -169,38 +208,14 @@
         ),
         send_llm, recv_llm,
     )
-    enc_start()
     for copy in own:
         copy.wait()
-    llm_start()
-
-    def text_local(j):
-        return pltpu.make_async_copy(
-            text.at[:, pl.ds(pl.multiple_of(j * 512 + c * 256, 256), 256)],
-            h0.at[c, :, pl.ds(j * 256, 256)],
-            text_l.at[j],
-        )
-
-    def text_other(j):
-        return remote(
-            text.at[:, pl.ds(pl.multiple_of(j * 512 + o * 256, 256), 256)],
-            h0.at[c, :, pl.ds(j * 256, 256)],
-            text_s.at[j], text_r.at[j], other,
-        )
-
-    def text_came(j):
-        return remote(
-            text.at[:, pl.ds(0, 256)],
-            h0.at[o, :, pl.ds(j * 256, 256)],
-            text_s.at[j], text_r.at[j], other,
-        )
 
     own_rows = pl.ds(pl.multiple_of(c * 48, 16), 48)
     other_rows = pl.ds(pl.multiple_of(o * 48, 16), 48)
     image_other = remote(img2.at[o], henc.at[own_rows], misc_s.at[0], misc_r.at[0], other)
-    marks_other = remote(ohb.at[c], ohb.at[c], misc_s.at[1], misc_r.at[1], other)
-
-    @pl.when(x == 0)
+
+    @pl.when(x == 2)
     def _():
         spread = lax.broadcasted_iota(jnp.int32, (256, 128), 0)
         lane = lax.broadcasted_iota(jnp.int32, (256, 128), 1)
@@ -213,6 +228,63 @@
             img2[b % 2, :, b // 2 * 128 : (b // 2 + 1) * 128] = block
         image_other.start()
         henc[own_rows, :] = img2[c]
+
+    @pl.when(x == 2)
+    def _():
+        for source in (0, 1):
+            for copy in gathered(source):
+                copy.wait_recv()
+        start, steps, finish = relay(
+            ((lambda s: E1.at[s],), (lambda s: E2.at[s],)), send_enc, recv_enc
+        )
+        start()
+        for step in steps:
+            step()
+        finish()
+
+    @pl.when(x == 3)
+    def _():
+        for copy in gathered(2):
+            copy.wait_recv()
+        start, steps, finish = relay(
+            (
+                (lambda s: E1.at[s], lambda s: C1.at[s]),
+                (lambda s: E2.at[s], lambda s: C2.at[s]),
+            ),
+            send_enc, recv_enc,
+        )
+        start()
+        for step in steps:
+            step()
+        finish()
+
+    llm_start()
+
+    def text_local(j):
+        return pltpu.make_async_copy(
+            text.at[:, pl.ds(pl.multiple_of(j * 512 + c * 256, 256), 256)],
+            h0.at[c, :, pl.ds(j * 256, 256)],
+            text_l.at[j],
+        )
+
+    def text_other(j):
+        return remote(
+            text.at[:, pl.ds(pl.multiple_of(j * 512 + o * 256, 256), 256)],
+            h0.at[c, :, pl.ds(j * 256, 256)],
+            text_s.at[j], text_r.at[j], other,
+        )
+
+    def text_came(j):
+        return remote(
+            text.at[:, pl.ds(0, 256)],
+            h0.at[o, :, pl.ds(j * 256, 256)],
+            text_s.at[j], text_r.at[j], other,
+        )
+
+    marks_other = remote(ohb.at[c], ohb.at[c], misc_s.at[1], misc_r.at[1], other)
+
+    @pl.when(x == 0)
+    def _():
         spot = jnp.full((1, 128), -1.0, F32)
         for m in range(3):
             j = lax.broadcasted_iota(jnp.int32, (16, 128), 0)
@@ -227,21 +299,6 @@
             text_local(j).start()
             text_other(j).start()
 
-    for step in enc_steps:
-        step()
-    enc_finish()
-
-    conn_start, conn_steps, conn_finish = relay(
-        ((lambda s: C1.at[s],), (lambda s: C2.at[s],)), send_enc, recv_conn
-    )
-
-    @pl.when(x == 3)
-    def _():
-        conn_start()
-        for step in conn_steps:
-            step()
-        conn_finish()
-
     def projected(slot, weight):
         h = henc[...]
         es[slot, :, 0:128] = matmul(h, weight.reshape(BLOCKS * 128, 128))
@@ -264,7 +321,7 @@
     def encoder(plane):
         @pl.when(x == plane)
         def _():
-            if plane == 0:
+            if plane == 2:
                 image_other.wait_send()
                 remote(
                     img2.at[c], henc.at[other_rows], misc_s.at[0], misc_r.at[0], other
@@ -273,15 +330,16 @@
                 passed.wait_recv()
 
             def layer(l, _):
-                activated = projected(l, E1[pl.ds(l * BLOCKS, BLOCKS)])
+                k, half = l // 2, lax.rem(l, 2)
+                activated = projected(half, E1[pl.ds(half * BLOCKS, BLOCKS), k])
                 for j in range(BLOCKS):
-                    branch = matmul(activated, E2[l * BLOCKS + j])
+                    branch = matmul(activated, E2[half * BLOCKS + j, k])
                     span = slice(j * 128, (j + 1) * 128)
                     henc[:, span] = (henc[:, span].astype(F32) + branch).astype(BF16)
                 return 0
 
-            lax.fori_loop(0, 2, layer, 0)
-            if plane < 3:
+            lax.fori_loop(0, 4, layer, 0)
+            if plane == 2:
                 passed.start()
             else:
                 latent = projected(0, C1[0:BLOCKS])[:, 0:64]
@@ -289,11 +347,10 @@
                     imgrows[0:96, j * 256 : (j + 1) * 256] = matmul(latent, C2[j]).astype(BF16)
                 pictures.start()
 
-    encoder(0)
-    turns = {int(len(llm_steps) * part): plane for plane, part in TURNS}
+    encoder(2)
     for number, step in enumerate(llm_steps):
-        if number in turns:
-            encoder(turns[number])
+        if number == TURN:
+            encoder(3)
         step()
     llm_finish()
 
@@ -312,9 +369,16 @@
     def _():
         pictures.wait_send()
 
-    @pl.when(x < 3)
+    @pl.when(x == 2)
     def _():
         passed.wait_send()
+
+    for source in range(3):
+
+        @pl.when(x == source)
+        def _():
+            for copy in gathered(source):
+                copy.wait_send()
 
     def cols(j):
         return slice(j * 256, (j + 1) * 256)
@@ -332,17 +396,18 @@
         )
         return silu(total[:, 0:512] * scale).astype(BF16)
 
-    def chunk(k, start, count, merge_last):
+    def flow(k, start, count, part):
+        base = pl.multiple_of(2 * start, 2 * count)
+        span = hin.at[pl.ds(base, 2 * count), pl.ds(part * 1024, 1024)]
+        return remote(span, span, flow_s.at[k, part], flow_r.at[k, part], x_next)
+
+    def chunk(k, start, count, merge_last, sent_last):
         size = 2 * count
         base = pl.multiple_of(2 * start, size)
         rows = pl.ds(pl.multiple_of(start, count), count)
         both = pl.ds(base, size)
         mine = pl.ds(pl.multiple_of(base + c * count, count), count)
         theirs = pl.ds(pl.multiple_of(base + o * count, count), count)
-
-        def flow(part):
-            span = hin.at[both, pl.ds(part * 1024, 1024)]
-            return remote(span, span, flow_s.at[k, part], flow_r.at[k, part], x_next)
 
         def emit():
             for j in range(BLOCKS):
@@ -364,7 +429,7 @@
 
             @pl.when(x > 0)
             def _():
-                flow(part).wait_recv()
+                flow(k, start, count, part).wait_recv()
 
             for j in range(4 * part, 4 * part + 4):
                 h = hin[both, cols(j)]
@@ -388,23 +453,14 @@
 
             @pl.when(x < 3)
             def _():
-                flow(part).start()
+                sent_last(part)
+                flow(k, start, count, part).start()
 
         @pl.when(z_hi == 1)
         def _():
             emit()
 
         merge_last()
-
-        def drain():
-            result(k, start, count).wait_send()
-
-            @pl.when(x < 3)
-            def _():
-                for part in range(4):
-                    flow(part).wait_send()
-
-        return drain
 
     def result(k, start, count):
         rows = pl.ds(pl.multiple_of(start, count), count)
@@ -422,32 +478,39 @@
             def _():
                 merge(k - 1, (k - 1) * 32, 32)
 
-        chunk(k, k * 32, 32, merge_last)
+        def sent_last(part):
+            @pl.when(k > 0)
+            def _():
+                flow(k - 1, (k - 1) * 32, 32, part).wait_send()
+
+        chunk(k, k * 32, 32, merge_last, sent_last)
         return 0
 
     lax.fori_loop(0, 5, full, 0)
-    half = [
-        chunk(5, 160, 16, lambda: merge(4, 128, 32)),
-        chunk(6, 176, 16, lambda: merge(5, 160, 16)),
-    ]
+    chunk(
+        5, 160, 16,
+        lambda: merge(4, 128, 32),
+        lambda part: flow(4, 128, 32, part).wait_send(),
+    )
+    chunk(
+        6, 176, 16,
+        lambda: merge(5, 160, 16),
+        lambda part: flow(5, 160, 16, part).wait_send(),
+    )
     merge(6, 176, 16)
 
     def drain(k, _):
         result(k, k * 32, 32).wait_send()
-
-        @pl.when(x < 3)
-        def _():
-            for part in range(4):
-                span = hin.at[
-                    pl.ds(pl.multiple_of(k * 64, 64), 64), pl.ds(part * 1024, 1024)
-                ]
-                remote(span, span, flow_s.at[k, part], flow_r.at[k, part], x_next).wait_send()
-
         return 0
 
     lax.fori_loop(0, 5, drain, 0)
-    for finish in half:
-        finish()
+    result(5, 160, 16).wait_send()
+    result(6, 176, 16).wait_send()
+
+    @pl.when(x < 3)
+    def _():
+        for part in range(4):
+            flow(6, 176, 16, part).wait_send()
 
 
 def local(text, image, positions, enc_in, enc_out, conn_in, conn_out, llm_in, llm_out):
@@ -462,10 +525,11 @@
         scratch_shapes=[
             pltpu.VMEM((32, 256, 512), BF16),
             pltpu.VMEM((32, 512, 256), BF16),
-            pltpu.VMEM((32, 128, 128), BF16),
-            pltpu.VMEM((32, 128, 128), BF16),
+            pltpu.VMEM((32, 2, 128, 128), BF16),
+            pltpu.VMEM((32, 2, 128, 128), BF16),
             pltpu.VMEM((32, 128, 128), BF16),
             pltpu.VMEM((32, 64, 256), BF16),
+            pltpu.VMEM((2, 128, 128), BF16),
             pltpu.VMEM((2, 192, 4096), BF16),
             pltpu.VMEM((2, 192, 128), BF16),
             pltpu.VMEM((2, 48, 2048), BF16),
@@ -480,9 +544,10 @@
             pltpu.VMEM((192, 4096), BF16),
             dma((3, 31)),
             dma((3, 32)),
-            dma((2, 31)),
-            dma((2, 32)),
-            dma((2, 32)),
+            dma((4, 31)),
+            dma((4, 32)),
+            dma((2,)),
+            dma((2, 2)),
             dma((2,)),
             dma((16,)),
             dma((16,)),

time: 289 us -> 245 us (0.85)
  Pallas kernels: 282 us -> 238 us
    pallas_call x1, Pallas kernels: 282 us -> 238 us  [local(): pl.pallas_call(kernel, out_shape=jax.ShapeDtypeStruct((192, 8192), BF16),...]
where the time goes in v3:
time: 245 us
  Pallas kernels  238 us (97%)
  local copies, waits for them, and re-layouts  6.74 us (3%)
    pallas_call x1, Pallas kernels, local(): pl.pallas_call(kernel, out_shape=jax.ShapeDtypeStruct((192, 8192), BF16),...  238 us
    unnamed x3, local copies, waits for them, and re-layouts  6.74 us

profile of v3, /device:TPU:7, one launch (start us, length us, event | category | flops | bytes accessed | tf_op | source)
XLA Modules:
  0.0 245.1 jit_solution(8793642108443250219)
XLA Ops:
  0.0 1.4 copy.11.conn_in
  1.4 1.5 copy.10
  2.9 238.4 %shard_map.91 = bf16[192,8192]{1,0:T(8,128)(2,1)} custom-call(bf16[192,8192]{1,0:T(8,128)(2,1)} %text.1, bf16[48,3200]{1,0:T(8,128)(2,1)} %image.1, s32[3,16]{1,0:T(4,128)} %positions.1, bf16[100,128]{1,0:T(8,128)(2,1)} %bitcast.9, bf16[128,100]{1,0:T(8,128)(2,1)} %bitcast.6, bf16[100,64]{1,0:T(8,128)(2,1)} %copy.11.conn_in, bf16[64,256]{1,0:T(8,128)(2,1)} %conn_out.1, ...), custom_call_target="tpu_custom_call" | custom-call | flops 14000000000 | bytes 16000000 | tf_op jit(solution)/shard_map/pallas_call | solution.py:520
  241.3 3.9 %copy.13 = bf16[1,192,8192]{2,1,0:T(8,128)(2,1)} copy(bf16[1,192,8192]{2,1,0:T(8,128)(2,1)} %bitcast.5) | data formatting | bytes 6291456

commit v4 on v3

--- a/solution.py
+++ b/solution.py
@@ -33,8 +33,9 @@
 def kernel(
     text, image, positions, enc_in, enc_out, conn_in, conn_out, wa, wb, out,
     A, B, E1, E2, C1, C2, ep, h0, ohb, img2, henc, imgrows, xs, xr, es, er, hin, osend, orecv,
+    zout, zin,
     send_llm, recv_llm, send_enc, recv_enc, gather_s, gather_r, own_sem, text_l, text_s, text_r,
-    misc_s, misc_r, x_s, x_r, xe_s, xe_r, flow_s, flow_r, out_s, out_r,
+    misc_s, misc_r, x_s, x_r, xe_s, xe_r, flow_s, flow_r, out_s, out_r, z_s, z_r,
 ):
     section = lax.axis_index("section")
     dp = lax.axis_index("dp")
@@ -53,6 +54,8 @@
     other = device(x, y, z, o)
     x_next = device(up(x, 1, 4), y, z, c)
     x_last = device(up(x, -1, 4), y, z, c)
+    x_far = device(up(x, 2, 4), y, z, c)
+    opposite = device(x, y, up(z, 4, 8), c)
 
     def remote(src, dst, ssem, rsem, to):
         return pltpu.make_async_remote_copy(
@@ -60,7 +63,7 @@
         )
 
     barrier = pltpu.get_barrier_semaphore()
-    for to in (y_up, y_down, z_up, z_down, other, x_next, x_last, device(up(x, 2, 4), y, z, c)):
+    for to in (y_up, y_down, z_up, z_down, other, x_next, x_last, x_far, opposite):
         pl.semaphore_signal(barrier, inc=1, device_id=to, device_id_type=MESH)
 
     own = [
@@ -83,7 +86,7 @@
         E1[me, 1] = ep[0]
         E2[me, 1] = ep[1]
 
-    pl.semaphore_wait(barrier, 8)
+    pl.semaphore_wait(barrier, 9)
 
     def gathered(source):
         to = device(max(2, source + 1), y, z, c)
@@ -386,34 +389,65 @@
     def folded(v):
         return v[:, 0:128] * v[:, 0:128] + v[:, 128:256] * v[:, 128:256]
 
-    def activation(slot, size, acc, squares):
-        mine = xs.at[slot, pl.ds(0, size)]
-        mine[:, 0:512] = acc
-        mine[:, 512:640] = squares
-        total = exchange(mine, xr.at[slot, pl.ds(0, size)], x_s, x_r, slot)
+    def activation(slot, acc, squares, meanwhile):
+        xs[slot, :, 0:512] = acc
+        xs[slot, :, 512:640] = squares
+        copy = remote(xs.at[slot], xr.at[slot], x_s.at[slot], x_r.at[slot], other)
+        copy.start()
+        meanwhile()
+        copy.wait()
+        total = xs[slot] + xr[slot]
         scale = lax.rsqrt(
             jnp.sum(total[:, 512:640], axis=-1, keepdims=True) * (1.0 / 8192) + EPSILON
         )
         return silu(total[:, 0:512] * scale).astype(BF16)
 
-    def flow(k, start, count, part):
-        base = pl.multiple_of(2 * start, 2 * count)
-        span = hin.at[pl.ds(base, 2 * count), pl.ds(part * 1024, 1024)]
+    def span_of(start):
+        return pl.ds(pl.multiple_of(start, 32), 32)
+
+    def flow(k, start, part):
+        span = hin.at[
+            pl.ds(pl.multiple_of(2 * start, 64), 64), pl.ds(part * 1024, 1024)
+        ]
         return remote(span, span, flow_s.at[k, part], flow_r.at[k, part], x_next)
 
-    def chunk(k, start, count, merge_last, sent_last):
-        size = 2 * count
-        base = pl.multiple_of(2 * start, size)
-        rows = pl.ds(pl.multiple_of(start, count), count)
-        both = pl.ds(base, size)
-        mine = pl.ds(pl.multiple_of(base + c * count, count), count)
-        theirs = pl.ds(pl.multiple_of(base + o * count, count), count)
-
-        def emit():
-            for j in range(BLOCKS):
-                out[rows, pl.ds(pl.multiple_of(j * 512 + c * 256, 256), 256)] = hin[mine, cols(j)]
-            osend[rows, :] = hin[theirs, :]
-            result(k, start, count).start()
+    def result(k, start):
+        rows = span_of(start)
+        return remote(osend.at[rows], orecv.at[rows], out_s.at[k], out_r.at[k], other)
+
+    def emit(k, start, source, base):
+        mine = pl.ds(pl.multiple_of(base + c * 32, 32), 32)
+        theirs = pl.ds(pl.multiple_of(base + o * 32, 32), 32)
+        rows = span_of(start)
+        osend[rows, :] = source[theirs, :]
+        result(k, start).start()
+        for j in range(BLOCKS):
+            out[rows, pl.ds(pl.multiple_of(j * 512 + c * 256, 256), 256)] = source[mine, cols(j)]
+
+    def merge(k, start):
+        result(k, start).wait_recv()
+        rows = span_of(start)
+        for j in range(BLOCKS):
+            out[rows, pl.ds(pl.multiple_of(j * 512 + o * 256, 256), 256)] = orecv[rows, cols(j)]
+
+    crossing = remote(zout, zin, z_s.at[0], z_r.at[0], opposite)
+
+    def chunk(k, start, halved, sent_last):
+        base = pl.multiple_of(2 * start, 64)
+        rows = span_of(start)
+        both = pl.ds(base, 64)
+
+        def give(layer):
+            @pl.when(z_hi == layer)
+            def _():
+                emit(k, start, hin, base)
+
+            if halved:
+
+                @pl.when(z_hi != layer)
+                def _():
+                    zout[...] = hin[both, :]
+                    crossing.start()
 
         @pl.when(x == 0)
         def _():
@@ -424,28 +458,23 @@
                 words = jnp.concatenate([h0[0, rows, cols(j)], h0[1, rows, cols(j)]], axis=0)
                 hin[both, cols(j)] = jnp.where(hit, placed, words.astype(F32)).astype(BF16)
 
-        acc, squares = jnp.zeros((size, 512), F32), jnp.zeros((size, 128), F32)
+        acc, squares = jnp.zeros((64, 512), F32), jnp.zeros((64, 128), F32)
         for part in range(4):
 
             @pl.when(x > 0)
             def _():
-                flow(k, start, count, part).wait_recv()
+                flow(k, start, part).wait_recv()
 
             for j in range(4 * part, 4 * part + 4):
                 h = hin[both, cols(j)]
                 acc, squares = acc + matmul(h, A[j]), squares + folded(h.astype(F32))
-        a = activation(0, size, acc, squares)
-        acc, squares = jnp.zeros((size, 512), F32), jnp.zeros((size, 128), F32)
+        a = activation(0, acc, squares, lambda: None)
+        acc, squares = jnp.zeros((64, 512), F32), jnp.zeros((64, 128), F32)
         for j in range(BLOCKS):
             h = (hin[both, cols(j)].astype(F32) + matmul(a, B[j])).astype(BF16)
             hin[both, cols(j)] = h
             acc, squares = acc + matmul(h, A[BLOCKS + j]), squares + folded(h.astype(F32))
-
-        @pl.when(z_hi == 0)
-        def _():
-            emit()
-
-        b = activation(1, size, acc, squares)
+        b = activation(1, acc, squares, lambda: give(0))
         for part in range(4):
             for j in range(4 * part, 4 * part + 4):
                 h = hin[both, cols(j)].astype(F32) + matmul(b, B[BLOCKS + j])
@@ -454,63 +483,54 @@
             @pl.when(x < 3)
             def _():
                 sent_last(part)
-                flow(k, start, count, part).start()
-
-        @pl.when(z_hi == 1)
+                flow(k, start, part).start()
+
+        give(1)
+
+    first = z_hi * 32
+    chunk(0, first, True, lambda part: None)
+
+    def shared(k, _):
+        def sent_last(part):
+            @pl.when(k == 1)
+            def _():
+                flow(0, first, part).wait_send()
+
+            @pl.when(k > 1)
+            def _():
+                flow(k - 1, 32 * k, part).wait_send()
+
+        chunk(k, 32 * k + 32, False, sent_last)
+
+        @pl.when(k == 1)
         def _():
-            emit()
-
-        merge_last()
-
-    def result(k, start, count):
-        rows = pl.ds(pl.multiple_of(start, count), count)
-        return remote(osend.at[rows], orecv.at[rows], out_s.at[k], out_r.at[k], other)
-
-    def merge(k, start, count):
-        result(k, start, count).wait_recv()
-        rows = pl.ds(pl.multiple_of(start, count), count)
-        for j in range(BLOCKS):
-            out[rows, pl.ds(pl.multiple_of(j * 512 + o * 256, 256), 256)] = orecv[rows, cols(j)]
-
-    def full(k, _):
-        def merge_last():
-            @pl.when(k > 0)
-            def _():
-                merge(k - 1, (k - 1) * 32, 32)
-
-        def sent_last(part):
-            @pl.when(k > 0)
-            def _():
-                flow(k - 1, (k - 1) * 32, 32, part).wait_send()
-
-        chunk(k, k * 32, 32, merge_last, sent_last)
+            merge(0, first)
+
+        @pl.when(k > 1)
+        def _():
+            merge(k - 1, 32 * k)
+
         return 0
 
-    lax.fori_loop(0, 5, full, 0)
-    chunk(
-        5, 160, 16,
-        lambda: merge(4, 128, 32),
-        lambda part: flow(4, 128, 32, part).wait_send(),
-    )
-    chunk(
-        6, 176, 16,
-        lambda: merge(5, 160, 16),
-        lambda part: flow(5, 160, 16, part).wait_send(),
-    )
-    merge(6, 176, 16)
+    lax.fori_loop(1, 5, shared, 0)
+    crossing.wait_recv()
+    emit(5, 32 - first, zin, 0)
+    merge(4, 160)
+    merge(5, 32 - first)
+    crossing.wait_send()
+    result(0, first).wait_send()
+    result(5, 32 - first).wait_send()
 
     def drain(k, _):
-        result(k, k * 32, 32).wait_send()
+        result(k, 32 * k + 32).wait_send()
         return 0
 
-    lax.fori_loop(0, 5, drain, 0)
-    result(5, 160, 16).wait_send()
-    result(6, 176, 16).wait_send()
+    lax.fori_loop(1, 5, drain, 0)
 
     @pl.when(x < 3)
     def _():
         for part in range(4):
-            flow(6, 176, 16, part).wait_send()
+            flow(4, 160, part).wait_send()
 
 
 def local(text, image, positions, enc_in, enc_out, conn_in, conn_out, llm_in, llm_out):
@@ -542,6 +562,8 @@
             pltpu.VMEM((384, 4096), BF16),
             pltpu.VMEM((192, 4096), BF16),
             pltpu.VMEM((192, 4096), BF16),
+            pltpu.VMEM((64, 4096), BF16),
+            pltpu.VMEM((64, 4096), BF16),
             dma((3, 31)),
             dma((3, 32)),
             dma((4, 31)),
@@ -558,10 +580,12 @@
             dma((2,)),
             dma((2,)),
             dma((2,)),
-            dma((7, 4)),
-            dma((7, 4)),
-            dma((7,)),
-            dma((7,)),
+            dma((5, 4)),
+            dma((5, 4)),
+            dma((6,)),
+            dma((6,)),
+            dma((1,)),
+            dma((1,)),
         ],
         compiler_params=pltpu.CompilerParams(
             collective_id=0, has_side_effects=True, vmem_limit_bytes=60 * 1024 * 1024

time: 245 us -> 231 us (0.943)
  Pallas kernels: 238 us -> 224 us
    pallas_call x1, Pallas kernels: 238 us -> 224 us  [local(): pl.pallas_call(kernel, out_shape=jax.ShapeDtypeStruct((192, 8192), BF16),...]
where the time goes in v4:
time: 231 us
  Pallas kernels  224 us (97%)
  local copies, waits for them, and re-layouts  6.74 us (3%)
    pallas_call x1, Pallas kernels, local(): pl.pallas_call(kernel, out_shape=jax.ShapeDtypeStruct((192, 8192), BF16),...  224 us
    unnamed x3, local copies, waits for them, and re-layouts  6.74 us

profile of v4, /device:TPU:7, one launch (start us, length us, event | category | flops | bytes accessed | tf_op | source)
XLA Modules:
  0.0 231.0 jit_solution(1268460812971134132)
XLA Ops:
  0.0 1.4 copy.11.conn_in
  1.4 1.5 copy.10
  2.9 224.2 %shard_map.91 = bf16[192,8192]{1,0:T(8,128)(2,1)} custom-call(bf16[192,8192]{1,0:T(8,128)(2,1)} %text.1, bf16[48,3200]{1,0:T(8,128)(2,1)} %image.1, s32[3,16]{1,0:T(4,128)} %positions.1, bf16[100,128]{1,0:T(8,128)(2,1)} %bitcast.9, bf16[128,100]{1,0:T(8,128)(2,1)} %bitcast.6, bf16[100,64]{1,0:T(8,128)(2,1)} %copy.11.conn_in, bf16[64,256]{1,0:T(8,128)(2,1)} %conn_out.1, ...), custom_call_target="tpu_custom_call" | custom-call | flops 14000000000 | bytes 16000000 | tf_op jit(solution)/shard_map/pallas_call | solution.py:540
  227.1 3.9 %copy.13 = bf16[1,192,8192]{2,1,0:T(8,128)(2,1)} copy(bf16[1,192,8192]{2,1,0:T(8,128)(2,1)} %bitcast.5) | data formatting | bytes 6291456

commit v5 on v4

--- a/solution.py
+++ b/solution.py
@@ -9,13 +9,17 @@
 MESH = pl.DeviceIdType.MESH
 F32 = jnp.float32
 BF16 = jnp.bfloat16
-SPLIT = 192
-TURN = 8
+SPLIT = 208
+TURN = 3
 BLOCKS = 16
 
 
 def gelu(v):
     return 0.5 * v * (1.0 + lax.erf(v * 0.7071067811865476))
+
+
+def matmul_t(a, b):
+    return lax.dot_general(a, b, (((1,), (1,)), ((), ())), preferred_element_type=F32)
 
 
 def silu(v):
@@ -33,9 +37,9 @@
 def kernel(
     text, image, positions, enc_in, enc_out, conn_in, conn_out, wa, wb, out,
     A, B, E1, E2, C1, C2, ep, h0, ohb, img2, henc, imgrows, xs, xr, es, er, hin, osend, orecv,
-    zout, zin,
+    zout, zin, zby,
     send_llm, recv_llm, send_enc, recv_enc, gather_s, gather_r, own_sem, text_l, text_s, text_r,
-    misc_s, misc_r, x_s, x_r, xe_s, xe_r, flow_s, flow_r, out_s, out_r, z_s, z_r,
+    misc_s, misc_r, x_s, x_r, xe_s, xe_r, flow_s, flow_r, out_s, out_r, z_s, z_r, by_s, by_r,
 ):
     section = lax.axis_index("section")
     dp = lax.axis_index("dp")
@@ -76,12 +80,12 @@
     ep[0] = blank
     ep[1] = blank
     ep[0, 0:100, :] = enc_in[...]
-    ep[1, :, 0:100] = enc_out[...]
+    ep[1, 0:100, :] = enc_out[...]
 
     @pl.when(x == 3)
     def _():
         C1[me] = blank
-        C1[me, 0:100, 0:64] = conn_in[...]
+        C1[me, 0:64, 0:100] = conn_in[...]
         C2[me] = conn_out[...]
         E1[me, 1] = ep[0]
         E2[me, 1] = ep[1]
@@ -302,9 +306,9 @@
             text_local(j).start()
             text_other(j).start()
 
-    def projected(slot, weight):
+    def projected(slot, product):
         h = henc[...]
-        es[slot, :, 0:128] = matmul(h, weight.reshape(BLOCKS * 128, 128))
+        es[slot, :, 0:128] = product(h)
         squares = jnp.zeros((96, 128), F32)
         for j in range(BLOCKS):
             part = h[:, j * 128 : (j + 1) * 128].astype(F32)
@@ -334,9 +338,10 @@
 
             def layer(l, _):
                 k, half = l // 2, lax.rem(l, 2)
-                activated = projected(half, E1[pl.ds(half * BLOCKS, BLOCKS), k])
+                weight = E1[pl.ds(half * BLOCKS, BLOCKS), k].reshape(BLOCKS * 128, 128)
+                activated = projected(half, lambda h: matmul(h, weight))
                 for j in range(BLOCKS):
-                    branch = matmul(activated, E2[half * BLOCKS + j, k])
+                    branch = matmul_t(activated, E2[half * BLOCKS + j, k])
                     span = slice(j * 128, (j + 1) * 128)
                     henc[:, span] = (henc[:, span].astype(F32) + branch).astype(BF16)
                 return 0
@@ -345,29 +350,55 @@
             if plane == 2:
                 passed.start()
             else:
-                latent = projected(0, C1[0:BLOCKS])[:, 0:64]
+
+                def to_latent(h):
+                    total = jnp.zeros((96, 128), F32)
+                    for j in range(BLOCKS):
+                        total += matmul_t(h[:, j * 128 : (j + 1) * 128], C1[j])
+                    return total
+
+                latent = projected(0, to_latent)[:, 0:64]
                 for j in range(BLOCKS):
                     imgrows[0:96, j * 256 : (j + 1) * 256] = matmul(latent, C2[j]).astype(BF16)
                 pictures.start()
+
+    def cols(j):
+        return slice(j * 256, (j + 1) * 256)
+
+    def first_state():
+        @pl.when(x == 0)
+        def _():
+            marks_other.wait_send()
+            remote(ohb.at[o], ohb.at[o], misc_s.at[1], misc_r.at[1], other).wait_recv()
+            for j in range(BLOCKS):
+                text_local(j).wait()
+                text_other(j).wait_send()
+                text_came(j).wait_recv()
+            imgrows[96:128, :] = jnp.zeros((32, BLOCKS * 256), BF16)
+            pictures.wait_recv()
+
+            def place(k, _):
+                rows = pl.ds(pl.multiple_of(32 * k, 32), 32)
+                both = pl.ds(pl.multiple_of(64 * k, 64), 64)
+                marks = jnp.concatenate([ohb[0, rows, :], ohb[1, rows, :]], axis=0)
+                hit = jnp.sum(marks.astype(F32), axis=-1, keepdims=True) > 0.5
+                for j in range(BLOCKS):
+                    placed = matmul(marks, imgrows[:, cols(j)])
+                    words = jnp.concatenate([h0[0, rows, cols(j)], h0[1, rows, cols(j)]], axis=0)
+                    hin[both, cols(j)] = jnp.where(hit, placed, words.astype(F32)).astype(BF16)
+                return 0
+
+            lax.fori_loop(0, 6, place, 0)
 
     encoder(2)
     for number, step in enumerate(llm_steps):
         if number == TURN:
             encoder(3)
+        if number == len(llm_steps) - 12:
+            first_state()
         step()
     llm_finish()
 
-    @pl.when(x == 0)
-    def _():
-        marks_other.wait_send()
-        remote(ohb.at[o], ohb.at[o], misc_s.at[1], misc_r.at[1], other).wait_recv()
-        for j in range(BLOCKS):
-            text_local(j).wait()
-            text_other(j).wait_send()
-            text_came(j).wait_recv()
-        imgrows[96:128, :] = jnp.zeros((32, BLOCKS * 256), BF16)
-        pictures.wait_recv()
-
     @pl.when(x == 3)
     def _():
         pictures.wait_send()
@@ -382,9 +413,6 @@
         def _():
             for copy in gathered(source):
                 copy.wait_send()
-
-    def cols(j):
-        return slice(j * 256, (j + 1) * 256)
 
     def folded(v):
         return v[:, 0:128] * v[:, 0:128] + v[:, 128:256] * v[:, 128:256]
@@ -430,7 +458,33 @@
         for j in range(BLOCKS):
             out[rows, pl.ds(pl.multiple_of(j * 512 + o * 256, 256), 256)] = orecv[rows, cols(j)]
 
-    crossing = remote(zout, zin, z_s.at[0], z_r.at[0], opposite)
+    def crossing(n):
+        k = min(n, 1)
+        span = pl.ds((0, 0, 2048)[n], (4096, 2048, 2048)[n])
+        return remote(zout.at[k, :, span], zin.at[k, :, span], z_s.at[n], z_r.at[n], opposite)
+
+    def leg(n, part):
+        near = pl.ds(part * 1024, 1024)
+        far = pl.ds(2048 + part * 1024, 1024)
+        src = (zout.at[1, :, far], zby.at[0, :, near], zby.at[1, :, near])[n]
+        dst = (zby.at[0, :, near], zby.at[1, :, near], zin.at[1, :, far])[n]
+        to = (x_next, opposite, x_last)[n]
+        return remote(src, dst, by_s.at[n, part], by_r.at[n, part], to)
+
+    def cross(k):
+        if k == 0:
+            crossing(0).start()
+            return
+        crossing(1).start()
+
+        @pl.when(x < 3)
+        def _():
+            crossing(2).start()
+
+        @pl.when(x == 3)
+        def _():
+            for part in range(2):
+                leg(0, part).start()
 
     def chunk(k, start, halved, sent_last):
         base = pl.multiple_of(2 * start, 64)
@@ -446,17 +500,8 @@
 
                 @pl.when(z_hi != layer)
                 def _():
-                    zout[...] = hin[both, :]
-                    crossing.start()
-
-        @pl.when(x == 0)
-        def _():
-            marks = jnp.concatenate([ohb[0, rows, :], ohb[1, rows, :]], axis=0)
-            hit = jnp.sum(marks.astype(F32), axis=-1, keepdims=True) > 0.5
-            for j in range(BLOCKS):
-                placed = matmul(marks, imgrows[:, cols(j)])
-                words = jnp.concatenate([h0[0, rows, cols(j)], h0[1, rows, cols(j)]], axis=0)
-                hin[both, cols(j)] = jnp.where(hit, placed, words.astype(F32)).astype(BF16)
+                    zout[k] = hin[both, :]
+                    cross(k)
 
         acc, squares = jnp.zeros((64, 512), F32), jnp.zeros((64, 128), F32)
         for part in range(4):
@@ -487,60 +532,90 @@
 
         give(1)
 
-    first = z_hi * 32
+    first = z_hi * 64
+    across_first = 64 - first
     chunk(0, first, True, lambda part: None)
+    chunk(1, first + 32, True, lambda part: flow(0, first, part).wait_send())
+    merge(0, first)
 
     def shared(k, _):
         def sent_last(part):
-            @pl.when(k == 1)
+            @pl.when(k == 2)
             def _():
-                flow(0, first, part).wait_send()
-
-            @pl.when(k > 1)
+                flow(1, first + 32, part).wait_send()
+
+            @pl.when(k > 2)
             def _():
-                flow(k - 1, 32 * k, part).wait_send()
-
-        chunk(k, 32 * k + 32, False, sent_last)
-
-        @pl.when(k == 1)
-        def _():
-            merge(0, first)
-
-        @pl.when(k > 1)
-        def _():
-            merge(k - 1, 32 * k)
+                flow(k - 1, 32 * k + 32, part).wait_send()
+
+        chunk(k, 32 * k + 64, False, sent_last)
+
+        @pl.when(k == 2)
+        def _():
+            merge(1, first + 32)
+
+        @pl.when(k > 2)
+        def _():
+            merge(k - 1, 32 * k + 32)
 
         return 0
 
-    lax.fori_loop(1, 5, shared, 0)
-    crossing.wait_recv()
-    emit(5, 32 - first, zin, 0)
-    merge(4, 160)
-    merge(5, 32 - first)
-    crossing.wait_send()
-    result(0, first).wait_send()
-    result(5, 32 - first).wait_send()
-
-    def drain(k, _):
-        result(k, 32 * k + 32).wait_send()
-        return 0
-
-    lax.fori_loop(1, 5, drain, 0)
+    lax.fori_loop(2, 4, shared, 0)
+    crossing(0).wait_recv()
+    emit(4, across_first, zin.at[0], 0)
+    merge(3, 160)
+    crossing(1).wait_recv()
 
     @pl.when(x < 3)
     def _():
+        crossing(2).wait_recv()
+
+    @pl.when(x == 3)
+    def _():
+        for part in range(2):
+            leg(2, part).wait_recv()
+
+    emit(5, across_first + 32, zin.at[1], 0)
+    for k in range(2):
+        merge(4 + k, across_first + 32 * k)
+        result(k, first + 32 * k).wait_send()
+        result(2 + k, 128 + 32 * k).wait_send()
+        result(4 + k, across_first + 32 * k).wait_send()
+        crossing(k).wait_send()
+
+    @pl.when(x < 3)
+    def _():
+        crossing(2).wait_send()
+
+    @pl.when(x == 3)
+    def _():
+        for part in range(2):
+            leg(0, part).wait_send()
+
+    @pl.when(x == 0)
+    def _():
+        for n in (0, 1):
+            for part in range(2):
+                leg(n, part).wait_recv()
+                leg(n + 1, part).start()
+        for n in (1, 2):
+            for part in range(2):
+                leg(n, part).wait_send()
+
+    @pl.when(x < 3)
+    def _():
         for part in range(4):
-            flow(4, 160, part).wait_send()
+            flow(3, 160, part).wait_send()
 
 
 def local(text, image, positions, enc_in, enc_out, conn_in, conn_out, llm_in, llm_out):
-    any_spec = pl.BlockSpec(memory_space=pl.ANY)
+    hbm_spec = pl.BlockSpec(memory_space=pltpu.HBM)
     vmem_spec = pl.BlockSpec(memory_space=pltpu.VMEM)
     dma = pltpu.SemaphoreType.DMA
     hidden = pl.pallas_call(
         kernel,
         out_shape=jax.ShapeDtypeStruct((192, 8192), BF16),
-        in_specs=[any_spec] + [vmem_spec] * 6 + [any_spec] * 2,
+        in_specs=[hbm_spec] + [vmem_spec] * 6 + [hbm_spec] * 2,
         out_specs=vmem_spec,
         scratch_shapes=[
             pltpu.VMEM((32, 256, 512), BF16),
@@ -562,8 +637,9 @@
             pltpu.VMEM((384, 4096), BF16),
             pltpu.VMEM((192, 4096), BF16),
             pltpu.VMEM((192, 4096), BF16),
-            pltpu.VMEM((64, 4096), BF16),
-            pltpu.VMEM((64, 4096), BF16),
+            pltpu.VMEM((2, 64, 4096), BF16),
+            pltpu.VMEM((2, 64, 4096), BF16),
+            pltpu.VMEM((2, 64, 2048), BF16),
             dma((3, 31)),
             dma((3, 32)),
             dma((4, 31)),
@@ -580,20 +656,24 @@
             dma((2,)),
             dma((2,)),
             dma((2,)),
-            dma((5, 4)),
-            dma((5, 4)),
+            dma((4, 4)),
+            dma((4, 4)),
             dma((6,)),
             dma((6,)),
-            dma((1,)),
-            dma((1,)),
+            dma((3,)),
+            dma((3,)),
+            dma((3, 2)),
+            dma((3, 2)),
         ],
         compiler_params=pltpu.CompilerParams(
-            collective_id=0, has_side_effects=True, vmem_limit_bytes=60 * 1024 * 1024
+            collective_id=0, has_side_effects=True, vmem_limit_bytes=50 * 1024 * 1024
         ),
         cost_estimate=pl.CostEstimate(
             flops=14_000_000_000, bytes_accessed=16_000_000, transcendentals=1_000_000
         ),
-    )(text, image, positions, enc_in[0], enc_out[0], conn_in, conn_out, llm_in[0], llm_out[0])
+    )(
+        text, image, positions, enc_in[0], enc_out[0].T, conn_in.T, conn_out, llm_in[0], llm_out[0]
+    )
     return hidden[None]
 
 

time: 231 us -> 216 us (0.935)
  Pallas kernels: 224 us -> 207 us
    pallas_call x1, Pallas kernels: 224 us -> 207 us  [local(): pl.pallas_call(kernel, out_shape=jax.ShapeDtypeStruct((192, 8192), BF16),...]
    unnamed x3 -> x17, local copies, waits for them, and re-layouts: 6.74 us -> 8.17 us
where the time goes in v5:
time: 216 us; the launch traced here: 215 us
  Pallas kernels  207 us (96%)
  local copies, waits for them, and re-layouts  8.17 us (4%)
    pallas_call x1, Pallas kernels, local(): pl.pallas_call(kernel, out_shape=jax.ShapeDtypeStruct((192, 8192), BF16),...  207 us
    unnamed x17, local copies, waits for them, and re-layouts  8.17 us

profile of v5, /device:TPU:7, one launch (start us, length us, event | category | flops | bytes accessed | tf_op | source)
XLA Modules:
  0.0 215.1 jit_solution(1747328467572027002)
XLA Ops:
  0.0 0.0 copy-start
  0.0 1.0 copy-done
  1.0 0.0 copy-start.1
  1.0 0.9 copy-done.1
  1.9 0.0 copy-start.2
  1.9 0.9 copy-done.2
  2.9 0.0 copy-start.3
  2.9 0.8 copy-done.3
  3.6 0.0 copy-start.4
  3.6 0.7 copy-done.4
  4.4 0.0 copy-start.5
  4.4 0.7 copy-done.5
  5.1 0.0 copy-start.6
  5.1 0.7 copy-done.6
  5.8 0.0 copy-start.7
  5.8 0.7 copy-done.7
  6.5 206.9 %shard_map.91 = bf16[192,8192]{1,0:T(8,128)(2,1)S(1)} custom-call(bf16[192,8192]{1,0:T(8,128)(2,1)} %text.1, bf16[48,3200]{1,0:T(8,128)(2,1)S(1)} %copy-done, s32[3,16]{1,0:T(4,128)S(1)} %copy-done.7, bf16[100,128]{1,0:T(8,128)(2,1)S(1)} %bitcast.11, bf16[100,128]{1,0:T(8,128)(2,1)S(1)} %bitcast.12, bf16[64,100]{1,0:T(8,128)(2,1)S(1)} %bitcast.13, ...), custom_call_target="tpu_custom_call" | custom-call | flops 14000000000 | bytes 16000000 | tf_op jit(solution)/shard_map/pallas_call | solution.py:615
  213.4 1.7 copy.11
Async XLA Ops:
  0.0 1.0 copy-start
  1.0 0.9 copy-start.1
  1.9 0.9 copy-start.2
  2.9 0.8 copy-start.3
  3.6 0.7 copy-start.4
  4.4 0.7 copy-start.5
  5.1 0.7 copy-start.6
  5.8 0.7 copy-start.7

commit v6 on v5

--- a/solution.py
+++ b/solution.py
@@ -377,7 +377,8 @@
             imgrows[96:128, :] = jnp.zeros((32, BLOCKS * 256), BF16)
             pictures.wait_recv()
 
-            def place(k, _):
+            def place(n, _):
+                k = n + jnp.where(n < 2, 2 * z_hi, 2)
                 rows = pl.ds(pl.multiple_of(32 * k, 32), 32)
                 both = pl.ds(pl.multiple_of(64 * k, 64), 64)
                 marks = jnp.concatenate([ohb[0, rows, :], ohb[1, rows, :]], axis=0)
@@ -388,7 +389,7 @@
                     hin[both, cols(j)] = jnp.where(hit, placed, words.astype(F32)).astype(BF16)
                 return 0
 
-            lax.fori_loop(0, 6, place, 0)
+            lax.fori_loop(0, 4, place, 0)
 
     encoder(2)
     for number, step in enumerate(llm_steps):
@@ -423,12 +424,12 @@
         copy = remote(xs.at[slot], xr.at[slot], x_s.at[slot], x_r.at[slot], other)
         copy.start()
         meanwhile()
-        copy.wait()
-        total = xs[slot] + xr[slot]
-        scale = lax.rsqrt(
-            jnp.sum(total[:, 512:640], axis=-1, keepdims=True) * (1.0 / 8192) + EPSILON
-        )
-        return silu(total[:, 0:512] * scale).astype(BF16)
+        copy.wait_recv()
+        squares += xr[slot, :, 512:640]
+        scale = lax.rsqrt(jnp.sum(squares, axis=-1, keepdims=True) * (1.0 / 8192) + EPSILON)
+        activated = silu((acc + xr[slot, :, 0:512]) * scale).astype(BF16)
+        copy.wait_send()
+        return activated
 
     def span_of(start):
         return pl.ds(pl.multiple_of(start, 32), 32)

time: 216 us -> 216 us (level)
  no operation moved by 1% of the time
where the time goes in v6:
time: 216 us; the launch traced here: 215 us
  Pallas kernels  207 us (96%)
  local copies, waits for them, and re-layouts  8.17 us (4%)
    pallas_call x1, Pallas kernels, local(): pl.pallas_call(kernel, out_shape=jax.ShapeDtypeStruct((192, 8192), BF16),...  207 us
    unnamed x17, local copies, waits for them, and re-layouts  8.17 us

profile of v6, /device:TPU:7, one launch (start us, length us, event | category | flops | bytes accessed | tf_op | source)
XLA Modules:
  0.0 215.4 jit_solution(3559288735337252582)
XLA Ops:
  0.0 0.0 copy-start
  0.0 1.0 copy-done
  1.0 0.0 copy-start.1
  1.0 0.9 copy-done.1
  1.9 0.0 copy-start.2
  1.9 0.9 copy-done.2
  2.9 0.0 copy-start.3
  2.9 0.8 copy-done.3
  3.6 0.0 copy-start.4
  3.6 0.7 copy-done.4
  4.4 0.0 copy-start.5
  4.4 0.7 copy-done.5
  5.1 0.0 copy-start.6
  5.1 0.7 copy-done.6
  5.8 0.0 copy-start.7
  5.8 0.7 copy-done.7
  6.5 207.3 %shard_map.91 = bf16[192,8192]{1,0:T(8,128)(2,1)S(1)} custom-call(bf16[192,8192]{1,0:T(8,128)(2,1)} %text.1, bf16[48,3200]{1,0:T(8,128)(2,1)S(1)} %copy-done, s32[3,16]{1,0:T(4,128)S(1)} %copy-done.7, bf16[100,128]{1,0:T(8,128)(2,1)S(1)} %bitcast.11, bf16[100,128]{1,0:T(8,128)(2,1)S(1)} %bitcast.12, bf16[64,100]{1,0:T(8,128)(2,1)S(1)} %bitcast.13, ...), custom_call_target="tpu_custom_call" | custom-call | flops 14000000000 | bytes 16000000 | tf_op jit(solution)/shard_map/pallas_call | solution.py:616
  213.8 1.7 copy.11
Async XLA Ops:
  0.0 1.0 copy-start
  1.0 0.9 copy-start.1
  1.9 0.9 copy-start.2
  2.9 0.8 copy-start.3
  3.6 0.7 copy-start.4
  4.4 0.7 copy-start.5
  5.1 0.7 copy-start.6
  5.8 0.7 copy-start.7
